TPU v7x, 128 devices: a whole 4x4x4 slice. The times are simulated.
128 devices in a mesh: tm: 16 (over z, y), rows: 8 (over x, core).
Axes of the slice: x: 4, y: 4, z: 4, core: 2. Of those that a mesh axis runs over, the one named last changes fastest.
Arguments:
- features: bfloat16 [64, 32, 64, 128], P('tm', 'rows'), may hold values from -6 to 6
- cotangent: bfloat16 [64, 32, 64, 128], P('tm', 'rows'), may hold values from -6 to 6
- first_kernel: bfloat16 [3, 3, 3, 128, 128], replicated, may hold values from -0.109375 to 0.109375
- second_kernel: bfloat16 [3, 3, 3, 128, 128], replicated, may hold values from -0.109375 to 0.109375
Outputs:
- block_out: bfloat16 [64, 32, 64, 128], P('tm', 'rows')
- grad_input: bfloat16 [64, 32, 64, 128], P('tm', 'rows')
- grad_first: float32 [3, 3, 3, 128, 128], P(None, None, None, None, 'tm')
- grad_second: float32 [3, 3, 3, 128, 128], P(None, None, None, None, 'tm')
All inputs are finite; a program needn't handle non-finite values.
Results may differ from a plain program's by a relative error of at most 0.0053.
Values may be sent and summed in bfloat16 or wider, within the bound.
A program may use at most 128 MiB of HBM per device.

v0:
```python
import functools
import math

import jax
import jax.numpy as jnp
from jax import lax
from jax.experimental import pallas as pl
from jax.experimental.pallas import tpu as pltpu
from jax.sharding import PartitionSpec as P

C = 128
MESH = pl.DeviceIdType.MESH
F32 = jnp.float32
BF16 = jnp.bfloat16


def zero_shift(values, step, width):
    if step == 0:
        return values
    rows = values.shape[0]
    column = lax.broadcasted_iota(jnp.int32, values.shape, 0) % width
    rolled = pltpu.roll(values, (-step) % rows, 0)
    edge = width - 1 if step > 0 else 0
    return jnp.where(column == edge, 0.0, rolled)


def kernel(
    geom, feat, cot, k1, k2, out_b, out_g, out_1, out_2,
    F, X, C_, H, G, W1, V2, W2, V1, slope, LT, PP, R0, S1, R1, S2, R2, S3, R3, D, ob, og, o1, o2,
    wsem, lsem, hsend, hrecv, s0, r0, s1, r1, s2, r2, s3, r3, s4, r4,
):
    nz, ny, nx, width, cells_all = geom
    ntm, nrows = nz * ny, nx * 2
    oc = C // ntm
    FR, RT = feat.shape[0], feat.shape[1]
    pairs = RT // 2
    cells = FR * RT * width
    tm, rows = lax.axis_index("tm"), lax.axis_index("rows")
    z, y = tm // ny, tm % ny
    x, core = rows // 2, rows % 2
    nf, ns = ny, nz
    first = (1 - core) * y + core * z
    second = (1 - core) * z + core * y

    def first_peer(d):
        return (1 - core) * (z * ny + (y + d) % ny) + core * (((z + d) % nz) * ny + y)

    def second_peer(d):
        return (1 - core) * (((z + d) % nz) * ny + y) + core * (z * ny + (y + d) % ny)

    def x_peer(d):
        return ((x + d) % nx) * 2 + core

    up, down = (tm + 1) % ntm, (tm + ntm - 1) % ntm
    right, left = (rows + 1) % nrows, (rows + nrows - 1) % nrows
    partner = x * 2 + 1 - core

    loads = {}
    count = [0]

    def load(name, src, dst):
        copy = pltpu.make_async_copy(src, dst, wsem.at[count[0]])
        count[0] += 1
        copy.start()
        loads.setdefault(name, []).append(copy)

    def arrived(name):
        for copy in loads[name]:
            copy.wait()

    load("F", feat, F.at[2 : 2 + FR, 1 : 1 + RT])
    load("C", cot, C_.at[0:FR, 1 : 1 + RT])

    def load_forward(name, src, W):
        for k in range(3):
            for o in range(2):
                load(name, src.at[:, :, k], W.at[k, :, o : o + 3, :, o * C : (o + 1) * C])

    def load_backward(name, src, V):
        for k in range(3):
            for o in range(2):
                for j in range(3):
                    at = o + 2 - j
                    load(name, src.at[:, j, k], V.at[k, :, o * C : (o + 1) * C, at * C : (at + 1) * C])

    load_forward("W1", k1, W1)
    load_backward("V2", k2, V2)
    load_forward("W2", k2, W2)
    load_backward("V1", k1, V1)

    peers = [(up, rows), (up, right), (up, left), (down, rows), (down, right), (down, left), (tm, right), (tm, left)]
    peers += [(first_peer(d), rows) for d in range(1, nf)]
    peers += [(second_peer(d), rows) for d in range(1, ns)]
    peers += [(tm, x_peer(d)) for d in range(1, nx)]
    barrier = pltpu.get_barrier_semaphore()
    for peer in peers:
        pl.semaphore_signal(barrier, inc=1, device_id=peer, device_id_type=MESH)
    pl.semaphore_wait(barrier, len(peers))

    def remote(src, dst, send, recv, peer):
        copy = pltpu.make_async_remote_copy(
            src_ref=src, dst_ref=dst, send_sem=send, recv_sem=recv, device_id=peer, device_id_type=MESH
        )
        copy.start()
        return copy

    sent = []

    def send_halo(which, src, at_f, at_r, dst, before):
        own = 2 if before else 0
        edge_src = slice(at_f + FR - 2, at_f + FR) if before else slice(at_f, at_f + 2)
        edge_dst = slice(0, 2) if before else slice(FR, FR + 2)
        ahead = up if before else down
        whole_src, whole_dst = slice(at_f, at_f + FR), slice(own, own + FR)
        last, start = slice(at_r + RT - 1, at_r + RT), slice(at_r, at_r + 1)
        low, high = slice(0, 1), slice(RT + 1, RT + 2)
        inner_src, inner_dst = slice(at_r, at_r + RT), slice(1, 1 + RT)
        plan = [
            (edge_src, inner_src, edge_dst, inner_dst, (ahead, rows)),
            (edge_src, last, edge_dst, low, (ahead, right)),
            (edge_src, start, edge_dst, high, (ahead, left)),
            (whole_src, last, whole_dst, low, (tm, right)),
            (whole_src, start, whole_dst, high, (tm, left)),
        ]
        copies = []
        for n, (sf, sr, df, dr, peer) in enumerate(plan):
            copies.append(remote(src.at[sf, sr], dst.at[df, dr], hsend.at[which, n], hrecv.at[which, n], peer))
        sent.extend(copies)
        return copies

    def receive_halo(copies, dst, before):
        for copy in copies:
            copy.wait_recv()

        @pl.when(tm == (0 if before else ntm - 1))
        def _():
            at = 0 if before else FR
            dst[at : at + 2] = jnp.zeros((2, RT + 2, width, C), BF16)

        @pl.when(rows == 0)
        def _():
            dst[:, 0] = jnp.zeros((FR + 2, width, C), BF16)

        @pl.when(rows == nrows - 1)
        def _():
            dst[:, RT + 1] = jnp.zeros((FR + 2, width, C), BF16)

    halo_f = send_halo(0, feat, 0, 0, F, True)
    halo_c = send_halo(1, cot, 0, 0, C_, False)

    for W in (W1, W2):
        W[:, :, 3, :, 0:C] = jnp.zeros((3, 3, C, C), BF16)
        W[:, :, 0, :, C : 2 * C] = jnp.zeros((3, 3, C, C), BF16)
    for V in (V1, V2):
        V[:, :, 0:C, 3 * C : 4 * C] = jnp.zeros((3, 3, C, C), BF16)
        V[:, :, C : 2 * C, 0:C] = jnp.zeros((3, 3, C, C), BF16)

    def window(field, lead):
        parts = []
        for pair in range(pairs):
            blocks = []
            for i in lead:
                for r in range(4):
                    blocks.append(field[i : i + FR, 2 * pair + r].reshape(FR * width, C))
            parts.append(jnp.concatenate(blocks, axis=1))
        return jnp.concatenate(parts, axis=0)

    def conv_forward(field, W):
        lhs = window(field, (0, 1, 2))
        total = None
        for k in (1, 0, 2):
            got = jnp.dot(lhs, W[k].reshape(12 * C, 2 * C), preferred_element_type=F32)
            got = zero_shift(got, k - 1, width)
            total = got if total is None else total + got
        return total

    def conv_backward(field, V):
        lhs = window(field, (2, 1, 0))
        total = None
        for k in (1, 0, 2):
            rhs = jnp.concatenate([V[k, i] for i in range(3)], axis=1)
            got = lax.dot_general(lhs, rhs, (((1,), (1,)), ((), ())), preferred_element_type=F32)
            got = zero_shift(got, 1 - k, width)
            total = got if total is None else total + got
        return total

    def put(dst, at_f, at_r, values):
        for pair in range(pairs):
            for o in range(2):
                part = values[pair * FR * width : (pair + 1) * FR * width, o * C : (o + 1) * C]
                dst[at_f : at_f + FR, at_r + 2 * pair + o] = part.reshape(FR, width, C).astype(dst.dtype)

    def get(src, at_f, at_r):
        parts = []
        for pair in range(pairs):
            blocks = [src[at_f : at_f + FR, at_r + 2 * pair + o].reshape(FR * width, C) for o in range(2)]
            parts.append(jnp.concatenate(blocks, axis=1))
        return jnp.concatenate(parts, axis=0).astype(F32)

    arrived("F")
    receive_halo(halo_f, F, True)
    for f in range(FR + 2):
        feats = F[f].astype(F32)
        X[f] = (feats * jax.nn.sigmoid(feats)).astype(BF16)
    arrived("W1")
    first_out = conv_forward(X, W1)
    sigma = jax.nn.sigmoid(first_out)
    put(H, 2, 1, first_out * sigma)
    slope[...] = sigma * (1.0 + first_out * (1.0 - sigma))
    halo_h = send_halo(2, H, 2, 1, H, True)

    arrived("C")
    receive_halo(halo_c, C_, False)
    arrived("V2")
    put(G, 0, 1, conv_backward(C_, V2) * slope[...])
    halo_g = send_halo(3, G, 0, 1, G, False)

    eye = (
        lax.broadcasted_iota(jnp.int32, (C, C), 0) == lax.broadcasted_iota(jnp.int32, (C, C), 1)
    ).astype(BF16)
    per_part = 7

    def kernel_gradient(g, own, field):
        grads = own[0:FR, 1 : 1 + RT].reshape(cells, C).astype(F32)
        for k in range(3):
            moved = zero_shift(grads, 1 - k, width).astype(BF16)
            turned = lax.dot_general(eye, moved, (((1,), (1,)), ((), ())), preferred_element_type=F32)
            LT[k * C : (k + 1) * C] = turned.astype(BF16)
        spots = [(i, j) for i in range(3) for j in range(3)]

        def block(i, j):
            return field[i : i + FR, j : j + RT].reshape(cells, C)

        def store(pair, a, b):
            part, slot = pair // per_part, pair % per_part
            both = jnp.concatenate([a.reshape(ntm, oc, C), b.reshape(ntm, oc, C)], axis=1).astype(BF16)
            for zz in range(nz):
                for yy in range(ny):
                    one, two = (yy, zz) if part == 0 else (zz, yy)
                    PP[g, part, one, two, slot] = both[zz * ny + yy]

        for m in range(5):
            group = spots[2 * m : 2 * m + 2]
            rhs = jnp.concatenate([block(i, j) for i, j in group], axis=1)
            got = jnp.dot(LT[...], rhs, preferred_element_type=F32)
            tail = []
            for n in range(len(group)):
                side = got[:, n * C : (n + 1) * C]
                store(2 * m + n, side[0:C], side[C : 2 * C])
                tail.append(side[2 * C : 3 * C])
            if len(tail) == 1:
                tail.append(jnp.zeros((C, C), F32))
            store(9 + m, tail[0], tail[1])

    def swap_start(g):
        return remote(PP.at[g, 1 - core], R0.at[g], s0.at[g], r0.at[g], (tm, partner))

    def swap_finish(g, copy):
        copy.wait_recv()
        S1[g] = (PP[g, core].astype(F32) + R0[g].astype(F32)).astype(BF16)
        copies = [
            remote(S1.at[g, (first + d) % nf], R1.at[g, d - 1], s1.at[g, d - 1], r1.at[g, d - 1], (first_peer(d), rows))
            for d in range(1, nf)
        ]
        sent.extend(copies)
        return copies

    def first_finish(g, copies):
        for copy in copies:
            copy.wait_recv()
        total = S1[g, first].astype(F32)
        for d in range(1, nf):
            total = total + R1[g, d - 1].astype(F32)
        S2[g] = total.astype(BF16)
        more = [
            remote(S2.at[g, (second + d) % ns], R2.at[g, d - 1], s2.at[g, d - 1], r2.at[g, d - 1], (second_peer(d), rows))
            for d in range(1, ns)
        ]
        sent.extend(more)
        return more

    def second_finish(g, copies):
        for copy in copies:
            copy.wait_recv()
        total = S2[g, second].astype(F32)
        for d in range(1, ns):
            total = total + R2[g, d - 1].astype(F32)
        S3[g] = total.astype(BF16)
        more = [
            remote(S3.at[g], R3.at[g, d - 1], s3.at[g, d - 1], r3.at[g, d - 1], (tm, x_peer(d)))
            for d in range(1, nx)
        ]
        sent.extend(more)
        return more

    scale = 1.0 / math.sqrt(cells_all)

    def third_finish(g, copies):
        for copy in copies:
            copy.wait_recv()
        total = S3[g].astype(F32)
        for d in range(1, nx):
            total = total + R3[g, d - 1].astype(F32)
        D[g, core] = total * scale
        copy = remote(D.at[g, core], D.at[g, core], s4.at[g], r4.at[g], (tm, partner))
        sent.append(copy)
        return copy

    kernel_gradient(0, G, X)
    swap_a = swap_start(0)
    receive_halo(halo_h, H, True)
    kernel_gradient(1, C_, H)
    swap_b = swap_start(1)
    sent.extend([swap_a, swap_b])
    one_a = swap_finish(0, swap_a)
    one_b = swap_finish(1, swap_b)

    arrived("W2")
    put(ob, 0, 0, get(F, 2, 1) + conv_forward(H, W2))
    write_b = pltpu.make_async_copy(ob, out_b, lsem.at[0])
    write_b.start()

    two_a = first_finish(0, one_a)
    two_b = first_finish(1, one_b)

    receive_halo(halo_g, G, False)
    arrived("V1")
    feats = get(F, 2, 1)
    sigma = jax.nn.sigmoid(feats)
    turn = sigma * (1.0 + feats * (1.0 - sigma))
    put(og, 0, 0, get(C_, 0, 1) + conv_backward(G, V1) * turn)
    write_g = pltpu.make_async_copy(og, out_g, lsem.at[1])
    write_g.start()

    three_a = second_finish(0, two_a)
    three_b = second_finish(1, two_b)
    four_a = third_finish(0, three_a)
    four_b = third_finish(1, three_b)

    def give(g, copy, buffer, out):
        copy.wait_recv()
        for pair in range(14):
            values = D[g, pair // per_part, pair % per_part]
            if pair < 9:
                taps = (3 * pair, 3 * pair + 1)
            else:
                taps = (6 * (pair - 9) + 2, 6 * (pair - 9) + 5)
            for n, tap in enumerate(taps):
                if tap < 27:
                    buffer[tap] = values[n * oc : (n + 1) * oc]
        write = pltpu.make_async_copy(buffer, out, lsem.at[2 + g])
        write.start()
        return write

    write_1 = give(0, four_a, o1, out_1)
    write_2 = give(1, four_b, o2, out_2)
    for copy in sent:
        copy.wait_send()
    for write in (write_b, write_g, write_1, write_2):
        write.wait()


def build(geom, features, cotangent, first_kernel, second_kernel):
    nz, ny, nx, width, cells_all = geom
    FR, RT = features.shape[0], features.shape[1]
    ntm = nz * ny
    oc = C // ntm
    tall = 2 * oc
    cells = FR * RT * width
    pad = pltpu.VMEM((FR + 2, RT + 2, width, C), BF16)
    forward = pltpu.VMEM((3, 3, 4, C, 2 * C), BF16)
    backward = pltpu.VMEM((3, 3, 2 * C, 4 * C), BF16)
    nf, ns = ny, nz
    scratch = [
        pad, pad, pad, pad, pad,
        forward, backward, forward, backward,
        pltpu.VMEM((cells // 2, 2 * C), F32),
        pltpu.VMEM((3 * C, cells), BF16),
        pltpu.VMEM((2, 2, nf, ns, 7, tall, C), BF16),
        pltpu.VMEM((2, nf, ns, 7, tall, C), BF16),
        pltpu.VMEM((2, nf, ns, 7, tall, C), BF16),
        pltpu.VMEM((2, nf - 1, ns, 7, tall, C), BF16),
        pltpu.VMEM((2, ns, 7, tall, C), BF16),
        pltpu.VMEM((2, ns - 1, 7, tall, C), BF16),
        pltpu.VMEM((2, 7, tall, C), BF16),
        pltpu.VMEM((2, nx - 1, 7, tall, C), BF16),
        pltpu.VMEM((2, 2, 7, tall, C), F32),
        pltpu.VMEM((FR, RT, width, C), BF16),
        pltpu.VMEM((FR, RT, width, C), BF16),
        pltpu.VMEM((27, oc, C), F32),
        pltpu.VMEM((27, oc, C), F32),
        pltpu.SemaphoreType.DMA((50,)),
        pltpu.SemaphoreType.DMA((4,)),
        pltpu.SemaphoreType.DMA((4, 5)),
        pltpu.SemaphoreType.DMA((4, 5)),
        pltpu.SemaphoreType.DMA((2,)),
        pltpu.SemaphoreType.DMA((2,)),
        pltpu.SemaphoreType.DMA((2, nf - 1)),
        pltpu.SemaphoreType.DMA((2, nf - 1)),
        pltpu.SemaphoreType.DMA((2, ns - 1)),
        pltpu.SemaphoreType.DMA((2, ns - 1)),
        pltpu.SemaphoreType.DMA((2, nx - 1)),
        pltpu.SemaphoreType.DMA((2, nx - 1)),
        pltpu.SemaphoreType.DMA((2,)),
        pltpu.SemaphoreType.DMA((2,)),
    ]
    anywhere = pl.BlockSpec(memory_space=pl.ANY)
    field = jax.ShapeDtypeStruct(features.shape, BF16)
    grads = jax.ShapeDtypeStruct((27, oc, C), F32)
    block_out, grad_input, g1, g2 = pl.pallas_call(
        functools.partial(kernel, geom),
        out_shape=(field, field, grads, grads),
        in_specs=[anywhere] * 4,
        out_specs=(anywhere,) * 4,
        scratch_shapes=scratch,
        compiler_params=pltpu.CompilerParams(
            collective_id=0, has_side_effects=True, vmem_limit_bytes=48 * 1024 * 1024
        ),
    )(features, cotangent, first_kernel, second_kernel)

    def place(values):
        return jnp.transpose(values.reshape(3, 3, 3, oc, C), (0, 1, 2, 4, 3))

    return block_out, grad_input, place(g1), place(g2)


def solution(mesh, sides=(4, 4, 4)):
    nz, ny, nx = sides

    def on_device(features, cotangent, first_kernel, second_kernel):
        width = features.shape[2]
        cells_all = features.shape[0] * features.shape[1] * width * nz * ny * nx * 2
        geom = (nz, ny, nx, width, cells_all)
        return build(geom, features, cotangent, first_kernel, second_kernel)

    return jax.shard_map(
        on_device,
        mesh=mesh,
        in_specs=(P("tm", "rows", None, None), P("tm", "rows", None, None), P(), P()),
        out_specs=(
            P("tm", "rows", None, None),
            P("tm", "rows", None, None),
            P(None, None, None, None, "tm"),
            P(None, None, None, None, "tm"),
        ),
        check_vma=False,
    )
```

profile of v0, /device:TPU:1, one launch (start us, length us, event | category | flops | bytes accessed | tf_op | source)
XLA Modules:
  0.0 52.1 jit_solution(13694434100722351641)
XLA Ops:
  0.6 0.0 copy-start
  0.6 1.2 %copy-done = bf16[3,3,3,128,128]{4,3,2,1,0:T(8,128)(2,1)S(1)} copy-done((bf16[3,3,3,128,128]{4,3,2,1,0:T(8,128)(2,1)S(1)}, bf16[3,3,3,128,128]{4,3,2,1,0:T(8,128)(2,1)}, u32[]{:S(2)}) %copy-start) | copy-done | bytes 884760
  1.8 0.0 copy-start.1
  1.8 1.2 %copy-done.1 = bf16[3,3,3,128,128]{4,3,2,1,0:T(8,128)(2,1)S(1)} copy-done((bf16[3,3,3,128,128]{4,3,2,1,0:T(8,128)(2,1)S(1)}, bf16[3,3,3,128,128]{4,3,2,1,0:T(8,128)(2,1)}, u32[]{:S(2)}) %copy-start.1) | copy-done | bytes 884760
  3.0 0.0 copy-start.2
  3.0 0.9 %copy-done.2 = bf16[4,4,64,128]{3,2,1,0:T(8,128)(2,1)S(1)} copy-done((bf16[4,4,64,128]{3,2,1,0:T(8,128)(2,1)S(1)}, bf16[4,4,64,128]{3,2,1,0:T(8,128)(2,1)}, u32[]{:S(2)}) %copy-start.2) | copy-done | bytes 262168
  3.9 0.0 copy-start.3
  3.9 0.9 %copy-done.3 = bf16[4,4,64,128]{3,2,1,0:T(8,128)(2,1)S(1)} copy-done((bf16[4,4,64,128]{3,2,1,0:T(8,128)(2,1)S(1)}, bf16[4,4,64,128]{3,2,1,0:T(8,128)(2,1)}, u32[]{:S(2)}) %copy-start.3) | copy-done | bytes 262168
  4.9 44.5 %shard_map.75 = (bf16[4,4,64,128]{3,2,1,0:T(8,128)(2,1)S(1)}, bf16[4,4,64,128]{3,2,1,0:T(8,128)(2,1)S(1)}, f32[27,8,128]{2,1,0:T(8,128)S(1)}, f32[27,8,128]{2,1,0:T(8,128)S(1)}) custom-call(bf16[4,4,64,128]{3,2,1,0:T(8,128)(2,1)S(1)} %copy-done.2, bf16[4,4,64,128]{3,2,1,0:T(8,128)(2,1)S(1)} %copy-done.3, bf16[3,3,3,128,128]{4,3,2,1,0:T(8,128)(2,1)S(1)} %copy-done, ...), custom_call_target="tpu_custom_call" | custom-call | tf_op jit(solution)/shard_map/pallas_call | solution.py:410
  49.4 0.7 %copy.12 = bf16[4,4,64,128]{3,2,1,0:T(8,128)(2,1)} copy(bf16[4,4,64,128]{3,2,1,0:T(8,128)(2,1)S(1)} %get-tuple-element.16) | data formatting | bytes 524288
  50.1 0.7 %copy.13 = bf16[4,4,64,128]{3,2,1,0:T(8,128)(2,1)} copy(bf16[4,4,64,128]{3,2,1,0:T(8,128)(2,1)S(1)} %get-tuple-element.17) | data formatting | bytes 524288
  50.8 0.6 %copy.14 = f32[3,3,3,128,8]{3,4,2,1,0:T(8,128)} copy(f32[3,3,3,128,8]{3,4,2,1,0:T(8,128)S(1)} %bitcast.7) | data formatting | bytes 221184
  51.5 0.6 %copy.15 = f32[3,3,3,128,8]{3,4,2,1,0:T(8,128)} copy(f32[3,3,3,128,8]{3,4,2,1,0:T(8,128)S(1)} %bitcast.6) | data formatting | bytes 221184
Async XLA Ops:
  0.6 1.2 %copy-start = (bf16[3,3,3,128,128]{4,3,2,1,0:T(8,128)(2,1)S(1)}, bf16[3,3,3,128,128]{4,3,2,1,0:T(8,128)(2,1)}, u32[]{:S(2)}) copy-start(bf16[3,3,3,128,128]{4,3,2,1,0:T(8,128)(2,1)} %k1.1) | copy-start | bytes 2654212
  1.8 1.2 %copy-start.1 = (bf16[3,3,3,128,128]{4,3,2,1,0:T(8,128)(2,1)S(1)}, bf16[3,3,3,128,128]{4,3,2,1,0:T(8,128)(2,1)}, u32[]{:S(2)}) copy-start(bf16[3,3,3,128,128]{4,3,2,1,0:T(8,128)(2,1)} %k2.1) | copy-start | bytes 2654212
  3.0 0.9 %copy-start.2 = (bf16[4,4,64,128]{3,2,1,0:T(8,128)(2,1)S(1)}, bf16[4,4,64,128]{3,2,1,0:T(8,128)(2,1)}, u32[]{:S(2)}) copy-start(bf16[4,4,64,128]{3,2,1,0:T(8,128)(2,1)} %feat.1) | copy-start | bytes 786436
  3.9 0.9 %copy-start.3 = (bf16[4,4,64,128]{3,2,1,0:T(8,128)(2,1)S(1)}, bf16[4,4,64,128]{3,2,1,0:T(8,128)(2,1)}, u32[]{:S(2)}) copy-start(bf16[4,4,64,128]{3,2,1,0:T(8,128)(2,1)} %cot.1) | copy-start | bytes 786436
where the time goes:
time: 52.4 us; the launch traced here: 52.1 us
  Pallas kernels  44.5 us (85%)
  local copies, waits for them, and re-layouts  6.92 us (13%)
  between operations  0.65 us (1%)
    pallas_call x1, Pallas kernels, build(): pl.pallas_call(functools.partial(kernel, geom), out_shape=(field, field,...  44.5 us
    unnamed x12, local copies, waits for them, and re-layouts  6.92 us

commit v1 on v0

--- a/solution.py
+++ b/solution.py
@@ -26,8 +26,8 @@
 
 def kernel(
     geom, feat, cot, k1, k2, out_b, out_g, out_1, out_2,
-    F, X, C_, H, G, W1, V2, W2, V1, slope, LT, PP, R0, S1, R1, S2, R2, S3, R3, D, ob, og, o1, o2,
-    wsem, lsem, hsend, hrecv, s0, r0, s1, r1, s2, r2, s3, r3, s4, r4,
+    F, X, C_, H, G, W1, V2, W2, V1, slope, LT, CT, CO, PP, R0, S1, R1, S2, R2, E, ob, og, o1, o2,
+    wsem, lsem, hsend, hrecv, s0, r0, s1, r1, s2, r2, s3, r3,
 ):
     nz, ny, nx, width, cells_all = geom
     ntm, nrows = nz * ny, nx * 2
@@ -38,18 +38,20 @@
     tm, rows = lax.axis_index("tm"), lax.axis_index("rows")
     z, y = tm // ny, tm % ny
     x, core = rows // 2, rows % 2
-    nf, ns = ny, nz
-    first = (1 - core) * y + core * z
-    second = (1 - core) * z + core * y
+    nf, plane = nx, nz * ny
+    first = (1 - core) * x + core * z
+    beside = (1 - core) * z + core * x
+    spot = beside * ny + y
 
     def first_peer(d):
-        return (1 - core) * (z * ny + (y + d) % ny) + core * (((z + d) % nz) * ny + y)
-
-    def second_peer(d):
-        return (1 - core) * (((z + d) % nz) * ny + y) + core * (z * ny + (y + d) % ny)
-
-    def x_peer(d):
-        return ((x + d) % nx) * 2 + core
+        return ((1 - core) * tm + core * (((z + d) % nz) * ny + y), (1 - core) * (((x + d) % nx) * 2) + core * rows)
+
+    def plane_spot(e):
+        return ((beside + e // ny) % nz) * ny + (y + e % ny) % ny
+
+    def plane_peer(e):
+        to, at = (beside + e // ny) % nz, (y + e % ny) % ny
+        return ((1 - core) * (to * ny + at) + core * (z * ny + at), (1 - core) * rows + core * (to * 2 + 1))
 
     up, down = (tm + 1) % ntm, (tm + ntm - 1) % ntm
     right, left = (rows + 1) % nrows, (rows + nrows - 1) % nrows
@@ -88,10 +90,10 @@
     load_forward("W2", k2, W2)
     load_backward("V1", k1, V1)
 
-    peers = [(up, rows), (up, right), (up, left), (down, rows), (down, right), (down, left), (tm, right), (tm, left)]
-    peers += [(first_peer(d), rows) for d in range(1, nf)]
-    peers += [(second_peer(d), rows) for d in range(1, ns)]
-    peers += [(tm, x_peer(d)) for d in range(1, nx)]
+    peers = [(up, rows), (up, right), (up, left), (down, rows), (down, right), (down, left)]
+    peers += [(tm, (rows + o) % nrows) for o in range(1, nrows)]
+    peers += [first_peer(d) for d in range(1, nf)]
+    peers += [plane_peer(e) for e in range(1, plane)]
     barrier = pltpu.get_barrier_semaphore()
     for peer in peers:
         pl.semaphore_signal(barrier, inc=1, device_id=peer, device_id_type=MESH)
@@ -155,6 +157,22 @@
         V[:, :, 0:C, 3 * C : 4 * C] = jnp.zeros((3, 3, C, C), BF16)
         V[:, :, C : 2 * C, 0:C] = jnp.zeros((3, 3, C, C), BF16)
 
+    chunk = 8 // nx
+    for g in range(2):
+        PP[g, 0, nx - 1, :, chunk - 1] = jnp.zeros((plane, 2 * oc, C), BF16)
+        PP[g, 1, :, (nx - 1) * ny :, chunk - 1] = jnp.zeros((nz, ny, 2 * oc, C), BF16)
+
+    def sigmoid(values):
+        return 0.5 * jnp.tanh(0.5 * values) + 0.5
+
+    def silu_into(f, r):
+        feats = F[f, r].astype(F32)
+        X[f, r] = (feats * sigmoid(feats)).astype(BF16)
+
+    arrived("F")
+    for f in range(2, 2 + FR):
+        silu_into(f, slice(1, 1 + RT))
+
     def window(field, lead):
         parts = []
         for pair in range(pairs):
@@ -197,73 +215,107 @@
             parts.append(jnp.concatenate(blocks, axis=1))
         return jnp.concatenate(parts, axis=0).astype(F32)
 
-    arrived("F")
     receive_halo(halo_f, F, True)
-    for f in range(FR + 2):
-        feats = F[f].astype(F32)
-        X[f] = (feats * jax.nn.sigmoid(feats)).astype(BF16)
+    for f in range(2):
+        silu_into(f, slice(0, RT + 2))
+    for f in range(2, 2 + FR):
+        silu_into(f, slice(0, 1))
+        silu_into(f, slice(RT + 1, RT + 2))
     arrived("W1")
     first_out = conv_forward(X, W1)
-    sigma = jax.nn.sigmoid(first_out)
+    sigma = sigmoid(first_out)
     put(H, 2, 1, first_out * sigma)
     slope[...] = sigma * (1.0 + first_out * (1.0 - sigma))
     halo_h = send_halo(2, H, 2, 1, H, True)
-
-    arrived("C")
-    receive_halo(halo_c, C_, False)
-    arrived("V2")
-    put(G, 0, 1, conv_backward(C_, V2) * slope[...])
-    halo_g = send_halo(3, G, 0, 1, G, False)
 
     eye = (
         lax.broadcasted_iota(jnp.int32, (C, C), 0) == lax.broadcasted_iota(jnp.int32, (C, C), 1)
     ).astype(BF16)
     per_part = 7
-
-    def kernel_gradient(g, own, field):
-        grads = own[0:FR, 1 : 1 + RT].reshape(cells, C).astype(F32)
+    spots = [(i, j) for i in range(3) for j in range(3)]
+
+    def turned(values):
+        return lax.dot_general(eye, values, (((1,), (1,)), ((), ())), preferred_element_type=F32).astype(BF16)
+
+    def store(g, pair, a, b):
+        part, slot = pair // per_part, pair % per_part
+        xs, at = slot // chunk, slot % chunk
+        both = jnp.concatenate([a.reshape(ntm, oc, C), b.reshape(ntm, oc, C)], axis=1).astype(BF16)
+        if part == 0:
+            PP[g, 0, xs, :, at] = both
+        else:
+            for zz in range(nz):
+                PP[g, 1, zz, xs * ny : (xs + 1) * ny, at] = both[zz * ny : (zz + 1) * ny]
+
+    def store_third(g, thirds):
+        thirds = thirds + [jnp.zeros((C, C), F32)]
+        for m in range(5):
+            store(g, 9 + m, thirds[2 * m], thirds[2 * m + 1])
+
+    def first_kernel_gradient():
+        grads = G[0:FR, 1 : 1 + RT].reshape(cells, C).astype(F32)
         for k in range(3):
-            moved = zero_shift(grads, 1 - k, width).astype(BF16)
-            turned = lax.dot_general(eye, moved, (((1,), (1,)), ((), ())), preferred_element_type=F32)
-            LT[k * C : (k + 1) * C] = turned.astype(BF16)
-        spots = [(i, j) for i in range(3) for j in range(3)]
-
-        def block(i, j):
-            return field[i : i + FR, j : j + RT].reshape(cells, C)
-
-        def store(pair, a, b):
-            part, slot = pair // per_part, pair % per_part
-            both = jnp.concatenate([a.reshape(ntm, oc, C), b.reshape(ntm, oc, C)], axis=1).astype(BF16)
-            for zz in range(nz):
-                for yy in range(ny):
-                    one, two = (yy, zz) if part == 0 else (zz, yy)
-                    PP[g, part, one, two, slot] = both[zz * ny + yy]
-
+            LT[k * C : (k + 1) * C] = turned(zero_shift(grads, 1 - k, width).astype(BF16))
+        thirds = []
         for m in range(5):
             group = spots[2 * m : 2 * m + 2]
-            rhs = jnp.concatenate([block(i, j) for i, j in group], axis=1)
+            rhs = jnp.concatenate([X[i : i + FR, j : j + RT].reshape(cells, C) for i, j in group], axis=1)
             got = jnp.dot(LT[...], rhs, preferred_element_type=F32)
-            tail = []
             for n in range(len(group)):
                 side = got[:, n * C : (n + 1) * C]
-                store(2 * m + n, side[0:C], side[C : 2 * C])
-                tail.append(side[2 * C : 3 * C])
-            if len(tail) == 1:
-                tail.append(jnp.zeros((C, C), F32))
-            store(9 + m, tail[0], tail[1])
-
-    def swap_start(g):
-        return remote(PP.at[g, 1 - core], R0.at[g], s0.at[g], r0.at[g], (tm, partner))
-
-    def swap_finish(g, copy):
-        copy.wait_recv()
-        S1[g] = (PP[g, core].astype(F32) + R0[g].astype(F32)).astype(BF16)
-        copies = [
-            remote(S1.at[g, (first + d) % nf], R1.at[g, d - 1], s1.at[g, d - 1], r1.at[g, d - 1], (first_peer(d), rows))
-            for d in range(1, nf)
-        ]
+                store(0, 2 * m + n, side[0:C], side[C : 2 * C])
+                thirds.append(side[2 * C : 3 * C])
+        store_third(0, thirds)
+
+    def second_kernel_gradient():
+        tall = (RT + 2) * width
+        for f in range(FR + 2):
+            CT[:, f * tall : (f + 1) * tall] = turned(C_[f].reshape(tall, C))
+            CO[:, f * RT * width : (f + 1) * RT * width] = turned(C_[f, 1 : 1 + RT].reshape(RT * width, C))
+        hidden = H[2 : 2 + FR, 1 : 1 + RT].reshape(cells, C).astype(F32)
+        rhs = jnp.concatenate([zero_shift(hidden, k - 1, width).astype(BF16) for k in range(3)], axis=1)
+
+        def turned_window(a, b):
+            if b == 1:
+                return CO[:, a * RT * width : (a + FR) * RT * width]
+            return jnp.concatenate(
+                [CT[:, f * tall + b * width : f * tall + (b + RT) * width] for f in range(a, a + FR)], axis=1
+            )
+
+        thirds = []
+        for i in range(3):
+            lhs = jnp.concatenate([turned_window(2 - i, 2 - j) for j in range(3)], axis=0)
+            got = jnp.dot(lhs, rhs, preferred_element_type=F32)
+            for j in range(3):
+                side = got[j * C : (j + 1) * C]
+                store(1, 3 * i + j, side[:, 0:C], side[:, C : 2 * C])
+                thirds.append(side[:, 2 * C : 3 * C])
+        store_third(1, thirds)
+
+    order = list(range(1, nf)) + [0]
+    other_first = (1 - core) * z + core * x
+
+    def pair_start(g):
+        copies = []
+        for d in order:
+            at = (other_first + d) % nf
+            copies.append(remote(PP.at[g, 1 - core, at], R0.at[g, at], s0.at[g, d], r0.at[g, d], (tm, partner)))
         sent.extend(copies)
         return copies
+
+    def pair_finish(g, copies):
+        more = []
+        for d, copy in zip(order, copies):
+            at = (first + d) % nf
+            pltpu.make_async_remote_copy(
+                src_ref=PP.at[g, core, at], dst_ref=R0.at[g, at], send_sem=s0.at[g, d], recv_sem=r0.at[g, d],
+                device_id=(tm, partner), device_id_type=MESH,
+            ).wait_recv()
+            S1[g, at] = (PP[g, core, at].astype(F32) + R0[g, at].astype(F32)).astype(BF16)
+            if d:
+                more.append(remote(S1.at[g, at], R1.at[g, d - 1], s1.at[g, d - 1], r1.at[g, d - 1], first_peer(d)))
+        sent.extend(more)
+        return more
 
     def first_finish(g, copies):
         for copy in copies:
@@ -273,74 +325,41 @@
             total = total + R1[g, d - 1].astype(F32)
         S2[g] = total.astype(BF16)
         more = [
-            remote(S2.at[g, (second + d) % ns], R2.at[g, d - 1], s2.at[g, d - 1], r2.at[g, d - 1], (second_peer(d), rows))
-            for d in range(1, ns)
+            remote(S2.at[g, plane_spot(e)], R2.at[g, e - 1], s2.at[g, e - 1], r2.at[g, e - 1], plane_peer(e))
+            for e in range(1, plane)
         ]
         sent.extend(more)
         return more
 
-    def second_finish(g, copies):
+    scale = 1.0 / math.sqrt(cells_all)
+
+    def plane_finish(g, copies):
         for copy in copies:
             copy.wait_recv()
-        total = S2[g, second].astype(F32)
-        for d in range(1, ns):
-            total = total + R2[g, d - 1].astype(F32)
-        S3[g] = total.astype(BF16)
+        total = S2[g, spot].astype(F32)
+        for e in range(1, plane):
+            total = total + R2[g, e - 1].astype(F32)
+        E[g, core, x] = (total * scale).astype(BF16)
         more = [
-            remote(S3.at[g], R3.at[g, d - 1], s3.at[g, d - 1], r3.at[g, d - 1], (tm, x_peer(d)))
-            for d in range(1, nx)
+            remote(
+                E.at[g, core, x], E.at[g, core, x], s3.at[g, o - 1], r3.at[g, o - 1], (tm, (rows + o) % nrows)
+            )
+            for o in range(1, nrows)
         ]
         sent.extend(more)
         return more
 
-    scale = 1.0 / math.sqrt(cells_all)
-
-    def third_finish(g, copies):
-        for copy in copies:
-            copy.wait_recv()
-        total = S3[g].astype(F32)
-        for d in range(1, nx):
-            total = total + R3[g, d - 1].astype(F32)
-        D[g, core] = total * scale
-        copy = remote(D.at[g, core], D.at[g, core], s4.at[g], r4.at[g], (tm, partner))
-        sent.append(copy)
-        return copy
-
-    kernel_gradient(0, G, X)
-    swap_a = swap_start(0)
-    receive_halo(halo_h, H, True)
-    kernel_gradient(1, C_, H)
-    swap_b = swap_start(1)
-    sent.extend([swap_a, swap_b])
-    one_a = swap_finish(0, swap_a)
-    one_b = swap_finish(1, swap_b)
-
-    arrived("W2")
-    put(ob, 0, 0, get(F, 2, 1) + conv_forward(H, W2))
-    write_b = pltpu.make_async_copy(ob, out_b, lsem.at[0])
-    write_b.start()
-
-    two_a = first_finish(0, one_a)
-    two_b = first_finish(1, one_b)
-
-    receive_halo(halo_g, G, False)
-    arrived("V1")
-    feats = get(F, 2, 1)
-    sigma = jax.nn.sigmoid(feats)
-    turn = sigma * (1.0 + feats * (1.0 - sigma))
-    put(og, 0, 0, get(C_, 0, 1) + conv_backward(G, V1) * turn)
-    write_g = pltpu.make_async_copy(og, out_g, lsem.at[1])
-    write_g.start()
-
-    three_a = second_finish(0, two_a)
-    three_b = second_finish(1, two_b)
-    four_a = third_finish(0, three_a)
-    four_b = third_finish(1, three_b)
-
-    def give(g, copy, buffer, out):
-        copy.wait_recv()
+    def give(g, copies, buffer, out):
+        for o in range(1, nrows):
+            giver = (rows + nrows - o) % nrows
+            block = E.at[g, giver % 2, giver // 2]
+            pltpu.make_async_remote_copy(
+                src_ref=block, dst_ref=block, send_sem=s3.at[g, o - 1], recv_sem=r3.at[g, o - 1],
+                device_id=(tm, (rows + o) % nrows), device_id_type=MESH,
+            ).wait_recv()
         for pair in range(14):
-            values = D[g, pair // per_part, pair % per_part]
+            slot = pair % per_part
+            values = E[g, pair // per_part, slot // chunk, slot % chunk].astype(F32)
             if pair < 9:
                 taps = (3 * pair, 3 * pair + 1)
             else:
@@ -352,12 +371,54 @@
         write.start()
         return write
 
-    write_1 = give(0, four_a, o1, out_1)
-    write_2 = give(1, four_b, o2, out_2)
+    arrived("C")
+    receive_halo(halo_c, C_, False)
+    second_kernel_gradient()
+    pair_b = pair_start(1)
+
+    arrived("V2")
+    put(G, 0, 1, conv_backward(C_, V2) * slope[...])
+    halo_g = send_halo(3, G, 0, 1, G, False)
+    one_b = pair_finish(1, pair_b)
+    first_kernel_gradient()
+    pair_a = pair_start(0)
+    two_b = first_finish(1, one_b)
+    one_a = pair_finish(0, pair_a)
+
+    receive_halo(halo_h, H, True)
+    arrived("W2")
+    put(ob, 0, 0, get(F, 2, 1) + conv_forward(H, W2))
+    write_b = pltpu.make_async_copy(ob, out_b, lsem.at[0])
+    write_b.start()
+
+    three_b = plane_finish(1, two_b)
+    two_a = first_finish(0, one_a)
+
+    receive_halo(halo_g, G, False)
+    arrived("V1")
+    feats = get(F, 2, 1)
+    sigma = sigmoid(feats)
+    turn = sigma * (1.0 + feats * (1.0 - sigma))
+    put(og, 0, 0, get(C_, 0, 1) + conv_backward(G, V1) * turn)
+    write_g = pltpu.make_async_copy(og, out_g, lsem.at[1])
+    write_g.start()
+
+    three_a = plane_finish(0, two_a)
+    write_2 = give(1, three_b, o2, out_2)
+    write_1 = give(0, three_a, o1, out_1)
     for copy in sent:
         copy.wait_send()
     for write in (write_b, write_g, write_1, write_2):
         write.wait()
+
+
+def hand_out(a, b, c, d, out_a, out_b, out_c, out_d, sems):
+    pairs = ((a, out_a), (b, out_b), (c, out_c), (d, out_d))
+    copies = [pltpu.make_async_copy(src, dst, sems.at[n]) for n, (src, dst) in enumerate(pairs)]
+    for copy in copies:
+        copy.start()
+    for copy in copies:
+        copy.wait()
 
 
 def build(geom, features, cotangent, first_kernel, second_kernel):
@@ -370,21 +431,21 @@
     pad = pltpu.VMEM((FR + 2, RT + 2, width, C), BF16)
     forward = pltpu.VMEM((3, 3, 4, C, 2 * C), BF16)
     backward = pltpu.VMEM((3, 3, 2 * C, 4 * C), BF16)
-    nf, ns = ny, nz
+    nf, plane, chunk = nx, nz * ny, 8 // nx
     scratch = [
         pad, pad, pad, pad, pad,
         forward, backward, forward, backward,
         pltpu.VMEM((cells // 2, 2 * C), F32),
         pltpu.VMEM((3 * C, cells), BF16),
-        pltpu.VMEM((2, 2, nf, ns, 7, tall, C), BF16),
-        pltpu.VMEM((2, nf, ns, 7, tall, C), BF16),
-        pltpu.VMEM((2, nf, ns, 7, tall, C), BF16),
-        pltpu.VMEM((2, nf - 1, ns, 7, tall, C), BF16),
-        pltpu.VMEM((2, ns, 7, tall, C), BF16),
-        pltpu.VMEM((2, ns - 1, 7, tall, C), BF16),
-        pltpu.VMEM((2, 7, tall, C), BF16),
-        pltpu.VMEM((2, nx - 1, 7, tall, C), BF16),
-        pltpu.VMEM((2, 2, 7, tall, C), F32),
+        pltpu.VMEM((C, (FR + 2) * (RT + 2) * width), BF16),
+        pltpu.VMEM((C, (FR + 2) * RT * width), BF16),
+        pltpu.VMEM((2, 2, nf, plane, chunk, tall, C), BF16),
+        pltpu.VMEM((2, nf, plane, chunk, tall, C), BF16),
+        pltpu.VMEM((2, nf, plane, chunk, tall, C), BF16),
+        pltpu.VMEM((2, nf - 1, plane, chunk, tall, C), BF16),
+        pltpu.VMEM((2, plane, chunk, tall, C), BF16),
+        pltpu.VMEM((2, plane - 1, chunk, tall, C), BF16),
+        pltpu.VMEM((2, 2, nx, chunk, tall, C), BF16),
         pltpu.VMEM((FR, RT, width, C), BF16),
         pltpu.VMEM((FR, RT, width, C), BF16),
         pltpu.VMEM((27, oc, C), F32),
@@ -393,18 +454,20 @@
         pltpu.SemaphoreType.DMA((4,)),
         pltpu.SemaphoreType.DMA((4, 5)),
         pltpu.SemaphoreType.DMA((4, 5)),
-        pltpu.SemaphoreType.DMA((2,)),
-        pltpu.SemaphoreType.DMA((2,)),
+        pltpu.SemaphoreType.DMA((2, nf)),
+        pltpu.SemaphoreType.DMA((2, nf)),
         pltpu.SemaphoreType.DMA((2, nf - 1)),
         pltpu.SemaphoreType.DMA((2, nf - 1)),
-        pltpu.SemaphoreType.DMA((2, ns - 1)),
-        pltpu.SemaphoreType.DMA((2, ns - 1)),
-        pltpu.SemaphoreType.DMA((2, nx - 1)),
-        pltpu.SemaphoreType.DMA((2, nx - 1)),
-        pltpu.SemaphoreType.DMA((2,)),
-        pltpu.SemaphoreType.DMA((2,)),
+        pltpu.SemaphoreType.DMA((2, plane - 1)),
+        pltpu.SemaphoreType.DMA((2, plane - 1)),
+        pltpu.SemaphoreType.DMA((2, 2 * nx - 1)),
+        pltpu.SemaphoreType.DMA((2, 2 * nx - 1)),
     ]
     anywhere = pl.BlockSpec(memory_space=pl.ANY)
+    features, cotangent, first_kernel, second_kernel = [
+        pltpu.with_memory_space_constraint(value, pltpu.HBM)
+        for value in (features, cotangent, first_kernel, second_kernel)
+    ]
     field = jax.ShapeDtypeStruct(features.shape, BF16)
     grads = jax.ShapeDtypeStruct((27, oc, C), F32)
     block_out, grad_input, g1, g2 = pl.pallas_call(
@@ -418,6 +481,15 @@
         ),
     )(features, cotangent, first_kernel, second_kernel)
 
+    block_out, grad_input, g1, g2 = pl.pallas_call(
+        hand_out,
+        out_shape=(field, field, grads, grads),
+        in_specs=[anywhere] * 4,
+        out_specs=(anywhere,) * 4,
+        scratch_shapes=[pltpu.SemaphoreType.DMA((4,))],
+        compiler_params=pltpu.CompilerParams(vmem_limit_bytes=8 * 1024 * 1024),
+    )(block_out, grad_input, g1, g2)
+
     def place(values):
         return jnp.transpose(values.reshape(3, 3, 3, oc, C), (0, 1, 2, 4, 3))
 

time: 52.4 us -> 47.3 us (0.903)
  local copies, waits for them, and re-layouts: 6.92 us -> 0 us
  Pallas kernels: 44.5 us -> 46.6 us
    unnamed x12 -> x0, local copies, waits for them, and re-layouts: 6.92 us -> none
    pallas_call x1, Pallas kernels: 44.5 us -> 45.7 us  [build(): pl.pallas_call(functools.partial(kernel, geom), out_shape=(field, field,...]
    pallas_call x0 -> x1, Pallas kernels: none -> 0.89 us  [build(): pl.pallas_call(hand_out, out_shape=(field, field, grads, grads), in_specs...]
where the time goes in v1:
time: 47.3 us; the launch traced here: 47.2 us
  Pallas kernels  46.6 us (99%)
  between operations  0.64 us (1%)
    pallas_call x1, Pallas kernels, build(): pl.pallas_call(functools.partial(kernel, geom), out_shape=(field, field,...  45.7 us

profile of v1, /device:TPU:1, one launch (start us, length us, event | category | flops | bytes accessed | tf_op | source)
XLA Modules:
  0.0 47.2 jit_solution(17710648372817476525)
XLA Ops:
  0.6 45.7 %shard_map.75 = (bf16[4,4,64,128]{3,2,1,0:T(8,128)(2,1)S(1)}, bf16[4,4,64,128]{3,2,1,0:T(8,128)(2,1)S(1)}, f32[27,8,128]{2,1,0:T(8,128)S(1)}, f32[27,8,128]{2,1,0:T(8,128)S(1)}) custom-call(bf16[4,4,64,128]{3,2,1,0:T(8,128)(2,1)} %feat.1, bf16[4,4,64,128]{3,2,1,0:T(8,128)(2,1)} %cot.1, bf16[3,3,3,128,128]{4,3,2,1,0:T(8,128)(2,1)} %k1.1, ...), custom_call_target="tpu_custom_call" | custom-call | tf_op jit(solution)/shard_map/pallas_call | solution.py:473
  46.3 0.9 %shard_map.76 = (bf16[4,4,64,128]{3,2,1,0:T(8,128)(2,1)}, bf16[4,4,64,128]{3,2,1,0:T(8,128)(2,1)}, f32[27,8,128]{2,1,0:T(8,128)}, f32[27,8,128]{2,1,0:T(8,128)}) custom-call(bf16[4,4,64,128]{3,2,1,0:T(8,128)(2,1)S(1)} %get-tuple-element.12.a, bf16[4,4,64,128]{3,2,1,0:T(8,128)(2,1)S(1)} %get-tuple-element.13.b, f32[27,8,128]{2,1,0:T(8,128)S(1)} %get-tuple-element.14.c, ...), custom_call_target="tpu_custom_call" | custom-call | tf_op jit(solution)/shard_map/pallas_call | solution.py:484

commit v2 on v1

v2 whole, which is shorter than its diff:
```python
import functools
import math

import jax
import jax.numpy as jnp
from jax import lax
from jax.experimental import pallas as pl
from jax.experimental.pallas import tpu as pltpu
from jax.sharding import PartitionSpec as P

C = 128
MESH = pl.DeviceIdType.MESH
F32 = jnp.float32
BF16 = jnp.bfloat16


def zero_shift(values, step, width):
    if step == 0:
        return values
    rows = values.shape[0]
    column = lax.broadcasted_iota(jnp.int32, values.shape, 0) % width
    rolled = pltpu.roll(values, (-step) % rows, 0)
    edge = width - 1 if step > 0 else 0
    return jnp.where(column == edge, 0.0, rolled)


def kernel(
    geom, feat, cot, k1, k2, out_b, out_g, out_1, out_2,
    F, X, C_, H, G, W1, V2, W2, V1, slope, early, LT, CT, CO, PP, R0, S1, R1, E,
    wsem, hsend, hrecv, s0, r0, s1, r1, s2, r2,
):
    nz, ny, nx, width, cells_all = geom
    ntm, nrows = nz * ny, nx * 2
    oc = C // ntm
    FR, RT = feat.shape[0], feat.shape[1]
    pairs = RT // 2
    cells = FR * RT * width
    tm, rows = lax.axis_index("tm"), lax.axis_index("rows")
    z, y = tm // ny, tm % ny
    x, core = rows // 2, rows % 2
    up, down = (tm + 1) % ntm, (tm + ntm - 1) % ntm
    right, left = (rows + 1) % nrows, (rows + nrows - 1) % nrows
    partner = x * 2 + 1 - core

    loads = {}
    count = [0]

    def load(name, src, dst):
        copy = pltpu.make_async_copy(src, dst, wsem.at[count[0]])
        count[0] += 1
        copy.start()
        loads.setdefault(name, []).append(copy)

    def arrived(name):
        for copy in loads[name]:
            copy.wait()

    load("F", feat, F.at[2 : 2 + FR, 1 : 1 + RT])
    load("C", cot, C_.at[0:FR, 1 : 1 + RT])

    def load_forward(name, src, W):
        for k in range(3):
            for o in range(2):
                load(name, src.at[:, :, k], W.at[k, :, o : o + 3, :, o * C : (o + 1) * C])

    def load_backward(name, src, V):
        for k in range(3):
            for o in range(2):
                for j in range(3):
                    at = o + 2 - j
                    load(name, src.at[:, j, k], V.at[k, :, o * C : (o + 1) * C, at * C : (at + 1) * C])

    load_forward("W1", k1, W1)
    load_backward("V2", k2, V2)
    load_forward("W2", k2, W2)
    load_backward("V1", k1, V1)

    peers = [(up, right), (up, left), (down, right), (down, left)]
    peers += [(tm, (rows + o) % nrows) for o in range(1, nrows)]

    def plane_peer(dz, dy):
        return (((z + dz) % nz) * ny + (y + dy) % ny, rows)

    offsets = [(dz, dy) for dz in list(range(1, nz)) + [0] for dy in range(ny) if (dz, dy) != (0, 0)]
    peers += [plane_peer(dz, dy) for dz, dy in offsets]
    barrier = pltpu.get_barrier_semaphore()
    for peer in peers:
        pl.semaphore_signal(barrier, inc=1, device_id=peer, device_id_type=MESH)
    pl.semaphore_wait(barrier, len(peers))

    def remote(src, dst, send, recv, peer):
        copy = pltpu.make_async_remote_copy(
            src_ref=src, dst_ref=dst, send_sem=send, recv_sem=recv, device_id=peer, device_id_type=MESH
        )
        copy.start()
        return copy

    sent = []

    def send_rows(which, src, at_f, at_r, dst, before):
        own = 2 if before else 0
        frames_src, frames_dst = slice(at_f, at_f + FR), slice(own, own + FR)
        plan = [
            (slice(at_r + RT - 1, at_r + RT), slice(0, 1), (tm, right)),
            (slice(at_r, at_r + 1), slice(RT + 1, RT + 2), (tm, left)),
        ]
        copies = []
        for n, (sr, dr, peer) in enumerate(plan):
            copies.append(
                remote(src.at[frames_src, sr], dst.at[frames_dst, dr], hsend.at[which, n], hrecv.at[which, n], peer)
            )
        sent.extend(copies)
        return copies

    def send_time(which, src, at_f, at_r, dst, before):
        frames_src = slice(at_f + FR - 2, at_f + FR) if before else slice(at_f, at_f + 2)
        frames_dst = slice(0, 2) if before else slice(FR, FR + 2)
        ahead = up if before else down
        plan = [
            (slice(at_r, at_r + RT), slice(1, 1 + RT), (ahead, rows)),
            (slice(at_r + RT - 1, at_r + RT), slice(0, 1), (ahead, right)),
            (slice(at_r, at_r + 1), slice(RT + 1, RT + 2), (ahead, left)),
        ]
        copies = []
        for n, (sr, dr, peer) in enumerate(plan):
            copies.append(
                remote(
                    src.at[frames_src, sr], dst.at[frames_dst, dr], hsend.at[which, 2 + n], hrecv.at[which, 2 + n], peer
                )
            )
        sent.extend(copies)
        return copies

    def clear_rims(dst, frames, count):
        @pl.when(rows == 0)
        def _():
            dst[frames, 0] = jnp.zeros((count, width, C), BF16)

        @pl.when(rows == nrows - 1)
        def _():
            dst[frames, RT + 1] = jnp.zeros((count, width, C), BF16)

    def receive_rows(copies, dst, before):
        for copy in copies:
            copy.wait_recv()
        own = 2 if before else 0
        clear_rims(dst, slice(own, own + FR), FR)

    def receive_time(copies, dst, before):
        for copy in copies:
            copy.wait_recv()
        at = 0 if before else FR

        @pl.when(tm == (0 if before else ntm - 1))
        def _():
            dst[at : at + 2] = jnp.zeros((2, RT + 2, width, C), BF16)

        clear_rims(dst, slice(at, at + 2), 2)

    rows_f = send_rows(0, feat, 0, 0, F, True)
    rows_c = send_rows(1, cot, 0, 0, C_, False)
    time_f = send_time(0, feat, 0, 0, F, True)
    time_c = send_time(1, cot, 0, 0, C_, False)

    for W in (W1, W2):
        W[:, :, 3, :, 0:C] = jnp.zeros((3, 3, C, C), BF16)
        W[:, :, 0, :, C : 2 * C] = jnp.zeros((3, 3, C, C), BF16)
    for V in (V1, V2):
        V[:, :, 0:C, 3 * C : 4 * C] = jnp.zeros((3, 3, C, C), BF16)
        V[:, :, C : 2 * C, 0:C] = jnp.zeros((3, 3, C, C), BF16)

    def sigmoid(values):
        return 0.5 * jnp.tanh(0.5 * values) + 0.5

    def silu_into(f, r):
        feats = F[f, r].astype(F32)
        X[f, r] = (feats * sigmoid(feats)).astype(BF16)

    arrived("F")
    for f in range(2, 2 + FR):
        silu_into(f, slice(1, 1 + RT))

    half = FR // 2

    def window(field, lead, lo, count):
        parts = []
        for pair in range(pairs):
            blocks = []
            for i in lead:
                for r in range(4):
                    blocks.append(field[lo + i : lo + i + count, 2 * pair + r].reshape(count * width, C))
            parts.append(jnp.concatenate(blocks, axis=1))
        return jnp.concatenate(parts, axis=0)

    def conv_forward(field, W, lo, count):
        lhs = window(field, (0, 1, 2), lo, count)
        total = None
        for k in (1, 0, 2):
            got = jnp.dot(lhs, W[k].reshape(12 * C, 2 * C), preferred_element_type=F32)
            got = zero_shift(got, k - 1, width)
            total = got if total is None else total + got
        return total

    def conv_backward(field, V, lo, count):
        lhs = window(field, (2, 1, 0), lo, count)
        total = None
        for k in (1, 0, 2):
            rhs = jnp.concatenate([V[k, i] for i in range(3)], axis=1)
            got = lax.dot_general(lhs, rhs, (((1,), (1,)), ((), ())), preferred_element_type=F32)
            got = zero_shift(got, 1 - k, width)
            total = got if total is None else total + got
        return total

    def put(dst, at_f, at_r, values):
        deep = values.shape[0] // pairs
        count = deep // width
        for pair in range(pairs):
            for o in range(2):
                part = values[pair * deep : (pair + 1) * deep, o * C : (o + 1) * C]
                dst[at_f : at_f + count, at_r + 2 * pair + o] = part.reshape(count, width, C).astype(dst.dtype)

    def get(src, at_f, at_r, count):
        parts = []
        for pair in range(pairs):
            blocks = [src[at_f : at_f + count, at_r + 2 * pair + o].reshape(count * width, C) for o in range(2)]
            parts.append(jnp.concatenate(blocks, axis=1))
        return jnp.concatenate(parts, axis=0).astype(F32)

    def first_conv(part):
        first_out = conv_forward(X, W1, part * half, half)
        sigma = sigmoid(first_out)
        put(H, 2 + part * half, 1, first_out * sigma)
        slope[part] = sigma * (1.0 + first_out * (1.0 - sigma))

    eye = (
        lax.broadcasted_iota(jnp.int32, (C, C), 0) == lax.broadcasted_iota(jnp.int32, (C, C), 1)
    ).astype(BF16)
    per_part = 7
    spots = [(i, j) for i in range(3) for j in range(3)]

    def turned(values):
        return lax.dot_general(eye, values, (((1,), (1,)), ((), ())), preferred_element_type=F32).astype(BF16)

    def store(g, pair, a, b):
        part, slot = pair // per_part, pair % per_part
        both = jnp.concatenate([a.reshape(nz, ny, oc, C), b.reshape(nz, ny, oc, C)], axis=2).astype(BF16)
        PP[g, part, :, :, slot] = both

    def store_third(g, thirds):
        thirds = thirds + [jnp.zeros((C, C), F32)]
        for m in range(5):
            store(g, 9 + m, thirds[2 * m], thirds[2 * m + 1])

    def first_kernel_gradient():
        grads = G[0:FR, 1 : 1 + RT].reshape(cells, C).astype(F32)
        for k in range(3):
            LT[k * C : (k + 1) * C] = turned(zero_shift(grads, 1 - k, width).astype(BF16))
        thirds = []
        for m in range(5):
            group = spots[2 * m : 2 * m + 2]
            rhs = jnp.concatenate([X[i : i + FR, j : j + RT].reshape(cells, C) for i, j in group], axis=1)
            got = jnp.dot(LT[...], rhs, preferred_element_type=F32)
            for n in range(len(group)):
                side = got[:, n * C : (n + 1) * C]
                store(0, 2 * m + n, side[0:C], side[C : 2 * C])
                thirds.append(side[2 * C : 3 * C])
        store_third(0, thirds)

    def second_kernel_gradient():
        tall = (RT + 2) * width
        for f in range(FR + 2):
            CT[:, f * tall : (f + 1) * tall] = turned(C_[f].reshape(tall, C))
            CO[:, f * RT * width : (f + 1) * RT * width] = turned(C_[f, 1 : 1 + RT].reshape(RT * width, C))
        hidden = H[2 : 2 + FR, 1 : 1 + RT].reshape(cells, C).astype(F32)
        rhs = jnp.concatenate([zero_shift(hidden, k - 1, width).astype(BF16) for k in range(3)], axis=1)

        def turned_window(a, b):
            if b == 1:
                return CO[:, a * RT * width : (a + FR) * RT * width]
            return jnp.concatenate(
                [CT[:, f * tall + b * width : f * tall + (b + RT) * width] for f in range(a, a + FR)], axis=1
            )

        thirds = []
        for i in range(3):
            lhs = jnp.concatenate([turned_window(2 - i, 2 - j) for j in range(3)], axis=0)
            got = jnp.dot(lhs, rhs, preferred_element_type=F32)
            for j in range(3):
                side = got[j * C : (j + 1) * C]
                store(1, 3 * i + j, side[:, 0:C], side[:, C : 2 * C])
                thirds.append(side[:, 2 * C : 3 * C])
        store_third(1, thirds)

    order = list(range(1, nz)) + [0]

    def pair_start(g):
        copies = []
        for dz in order:
            at = (z + dz) % nz
            copies.append(remote(PP.at[g, 1 - core, at], R0.at[g, at], s0.at[g, dz], r0.at[g, dz], (tm, partner)))
        sent.extend(copies)
        return copies

    def pair_finish(g, copies):
        more = []
        for dz, copy in zip(order, copies):
            copy.wait_recv()
            at = (z + dz) % nz
            S1[g, at] = (PP[g, core, at].astype(F32) + R0[g, at].astype(F32)).astype(BF16)
            for dy in range(ny):
                if (dz, dy) == (0, 0):
                    continue
                e = dz * ny + dy - 1
                more.append(
                    remote(S1.at[g, at, (y + dy) % ny], R1.at[g, e], s1.at[g, e], r1.at[g, e], plane_peer(dz, dy))
                )
        sent.extend(more)
        return more

    scale = 1.0 / math.sqrt(cells_all)

    def plane_finish(g, copies):
        for copy in copies:
            copy.wait_recv()
        total = S1[g, z, y].astype(F32)
        for e in range(ntm - 1):
            total = total + R1[g, e].astype(F32)
        E[g, core, x] = total.astype(BF16)
        more = [
            remote(
                E.at[g, core, x], E.at[g, core, x], s2.at[g, o - 1], r2.at[g, o - 1], (tm, (rows + o) % nrows)
            )
            for o in range(1, nrows)
        ]
        sent.extend(more)
        return more

    def give(g, out):
        for o in range(1, nrows):
            giver = (rows + nrows - o) % nrows
            block = E.at[g, giver % 2, giver // 2]
            pltpu.make_async_remote_copy(
                src_ref=block, dst_ref=block, send_sem=s2.at[g, o - 1], recv_sem=r2.at[g, o - 1],
                device_id=(tm, (rows + o) % nrows), device_id_type=MESH,
            ).wait_recv()
        for pair in range(14):
            part, slot = pair // per_part, pair % per_part
            values = E[g, part, 0, slot].astype(F32)
            for at in range(1, nx):
                values = values + E[g, part, at, slot].astype(F32)
            values = values * scale
            if pair < 9:
                taps = (3 * pair, 3 * pair + 1)
            else:
                taps = (6 * (pair - 9) + 2, 6 * (pair - 9) + 5)
            for n, tap in enumerate(taps):
                if tap < 27:
                    out[tap] = values[n * oc : (n + 1) * oc]

    receive_rows(rows_f, F, True)
    for f in range(2, 2 + FR):
        silu_into(f, slice(0, 1))
        silu_into(f, slice(RT + 1, RT + 2))
    arrived("W1")
    first_conv(1)
    time_h = send_time(2, H, 2, 1, H, True)
    arrived("C")
    receive_rows(rows_c, C_, False)
    arrived("V2")
    early[...] = conv_backward(C_, V2, 0, half)

    receive_time(time_f, F, True)
    for f in range(2):
        silu_into(f, slice(0, RT + 2))
    first_conv(0)
    rows_h = send_rows(2, H, 2, 1, H, True)
    put(G, 0, 1, early[...] * slope[0])
    time_g = send_time(3, G, 0, 1, G, False)

    receive_time(time_c, C_, False)
    second_kernel_gradient()
    pair_b = pair_start(1)
    put(G, half, 1, conv_backward(C_, V2, half, half) * slope[1])
    rows_g = send_rows(3, G, 0, 1, G, False)
    plane_b = pair_finish(1, pair_b)
    first_kernel_gradient()
    pair_a = pair_start(0)
    plane_a = pair_finish(0, pair_a)

    receive_rows(rows_h, H, True)
    receive_time(time_h, H, True)
    arrived("W2")
    put(out_b, 0, 0, get(F, 2, 1, FR) + conv_forward(H, W2, 0, FR))

    rows_b = plane_finish(1, plane_b)

    receive_rows(rows_g, G, False)
    receive_time(time_g, G, False)
    arrived("V1")
    feats = get(F, 2, 1, FR)
    sigma = sigmoid(feats)
    turn = sigma * (1.0 + feats * (1.0 - sigma))
    put(out_g, 0, 0, get(C_, 0, 1, FR) + conv_backward(G, V1, 0, FR) * turn)

    rows_a = plane_finish(0, plane_a)
    give(1, out_2)
    give(0, out_1)
    for copy in sent:
        copy.wait_send()


def hand_out(a, b, c, d, out_a, out_b, out_c, out_d, sems):
    pairs = ((a, out_a), (b, out_b), (c, out_c), (d, out_d))
    copies = [pltpu.make_async_copy(src, dst, sems.at[n]) for n, (src, dst) in enumerate(pairs)]
    for copy in copies:
        copy.start()
    for copy in copies:
        copy.wait()


def build(geom, features, cotangent, first_kernel, second_kernel):
    nz, ny, nx, width, cells_all = geom
    FR, RT = features.shape[0], features.shape[1]
    ntm = nz * ny
    oc = C // ntm
    tall = 2 * oc
    cells = FR * RT * width
    pad = pltpu.VMEM((FR + 2, RT + 2, width, C), BF16)
    forward = pltpu.VMEM((3, 3, 4, C, 2 * C), BF16)
    backward = pltpu.VMEM((3, 3, 2 * C, 4 * C), BF16)
    block = (7, tall, C)
    scratch = [
        pad, pad, pad, pad, pad,
        forward, backward, forward, backward,
        pltpu.VMEM((2, cells // 4, 2 * C), F32),
        pltpu.VMEM((cells // 4, 2 * C), F32),
        pltpu.VMEM((3 * C, cells), BF16),
        pltpu.VMEM((C, (FR + 2) * (RT + 2) * width), BF16),
        pltpu.VMEM((C, (FR + 2) * RT * width), BF16),
        pltpu.VMEM((2, 2, nz, ny) + block, BF16),
        pltpu.VMEM((2, nz, ny) + block, BF16),
        pltpu.VMEM((2, nz, ny) + block, BF16),
        pltpu.VMEM((2, ntm - 1) + block, BF16),
        pltpu.VMEM((2, 2, nx) + block, BF16),
        pltpu.SemaphoreType.DMA((50,)),
        pltpu.SemaphoreType.DMA((4, 5)),
        pltpu.SemaphoreType.DMA((4, 5)),
        pltpu.SemaphoreType.DMA((2, nz)),
        pltpu.SemaphoreType.DMA((2, nz)),
        pltpu.SemaphoreType.DMA((2, ntm - 1)),
        pltpu.SemaphoreType.DMA((2, ntm - 1)),
        pltpu.SemaphoreType.DMA((2, 2 * nx - 1)),
        pltpu.SemaphoreType.DMA((2, 2 * nx - 1)),
    ]
    anywhere = pl.BlockSpec(memory_space=pl.ANY)
    features, cotangent, first_kernel, second_kernel = [
        pltpu.with_memory_space_constraint(value, pltpu.HBM)
        for value in (features, cotangent, first_kernel, second_kernel)
    ]
    field = jax.ShapeDtypeStruct(features.shape, BF16)
    grads = jax.ShapeDtypeStruct((27, oc, C), F32)
    block_out, grad_input, g1, g2 = pl.pallas_call(
        functools.partial(kernel, geom),
        out_shape=(field, field, grads, grads),
        in_specs=[anywhere] * 4,
        out_specs=(pl.BlockSpec(memory_space=pltpu.VMEM),) * 4,
        scratch_shapes=scratch,
        compiler_params=pltpu.CompilerParams(
            collective_id=0, has_side_effects=True, vmem_limit_bytes=48 * 1024 * 1024
        ),
    )(features, cotangent, first_kernel, second_kernel)

    block_out, grad_input, g1, g2 = pl.pallas_call(
        hand_out,
        out_shape=(field, field, grads, grads),
        in_specs=[anywhere] * 4,
        out_specs=(anywhere,) * 4,
        scratch_shapes=[pltpu.SemaphoreType.DMA((4,))],
        compiler_params=pltpu.CompilerParams(vmem_limit_bytes=8 * 1024 * 1024),
    )(block_out, grad_input, g1, g2)

    def place(values):
        return jnp.transpose(values.reshape(3, 3, 3, oc, C), (0, 1, 2, 4, 3))

    return block_out, grad_input, place(g1), place(g2)


def solution(mesh, sides=(4, 4, 4)):
    nz, ny, nx = sides

    def on_device(features, cotangent, first_kernel, second_kernel):
        width = features.shape[2]
        cells_all = features.shape[0] * features.shape[1] * width * nz * ny * nx * 2
        geom = (nz, ny, nx, width, cells_all)
        return build(geom, features, cotangent, first_kernel, second_kernel)

    return jax.shard_map(
        on_device,
        mesh=mesh,
        in_specs=(P("tm", "rows", None, None), P("tm", "rows", None, None), P(), P()),
        out_specs=(
            P("tm", "rows", None, None),
            P("tm", "rows", None, None),
            P(None, None, None, None, "tm"),
            P(None, None, None, None, "tm"),
        ),
        check_vma=False,
    )
```

time: 47.3 us -> 41.6 us (0.88)
  Pallas kernels: 46.6 us -> 40.8 us
    pallas_call x1, Pallas kernels: 45.7 us -> 39.9 us  [build(): pl.pallas_call(functools.partial(kernel, geom), out_shape=(field, field,...]
where the time goes in v2:
time: 41.6 us; the launch traced here: 41.5 us
  Pallas kernels  40.8 us (98%)
  between operations  0.64 us (2%)
    pallas_call x1, Pallas kernels, build(): pl.pallas_call(functools.partial(kernel, geom), out_shape=(field, field,...  39.9 us
    pallas_call x1, Pallas kernels, build(): pl.pallas_call(hand_out, out_shape=(field, field, grads, grads), in_specs...  0.89 us

profile of v2, /device:TPU:1, one launch (start us, length us, event | category | flops | bytes accessed | tf_op | source)
XLA Modules:
  0.0 41.5 jit_solution(5840522537374906137)
XLA Ops:
  0.6 39.9 %shard_map.75 = (bf16[4,4,64,128]{3,2,1,0:T(8,128)(2,1)S(1)}, bf16[4,4,64,128]{3,2,1,0:T(8,128)(2,1)S(1)}, f32[27,8,128]{2,1,0:T(8,128)S(1)}, f32[27,8,128]{2,1,0:T(8,128)S(1)}) custom-call(bf16[4,4,64,128]{3,2,1,0:T(8,128)(2,1)} %feat.1, bf16[4,4,64,128]{3,2,1,0:T(8,128)(2,1)} %cot.1, bf16[3,3,3,128,128]{4,3,2,1,0:T(8,128)(2,1)} %k1.1, ...), custom_call_target="tpu_custom_call" | custom-call | tf_op jit(solution)/shard_map/pallas_call | solution.py:462
  40.6 0.9 %shard_map.76 = (bf16[4,4,64,128]{3,2,1,0:T(8,128)(2,1)}, bf16[4,4,64,128]{3,2,1,0:T(8,128)(2,1)}, f32[27,8,128]{2,1,0:T(8,128)}, f32[27,8,128]{2,1,0:T(8,128)}) custom-call(bf16[4,4,64,128]{3,2,1,0:T(8,128)(2,1)S(1)} %get-tuple-element.12.a, bf16[4,4,64,128]{3,2,1,0:T(8,128)(2,1)S(1)} %get-tuple-element.13.b, f32[27,8,128]{2,1,0:T(8,128)S(1)} %get-tuple-element.14.c, ...), custom_call_target="tpu_custom_call" | custom-call | tf_op jit(solution)/shard_map/pallas_call | solution.py:473

commit v3 on v2

--- a/solution.py
+++ b/solution.py
@@ -235,42 +235,57 @@
     eye = (
         lax.broadcasted_iota(jnp.int32, (C, C), 0) == lax.broadcasted_iota(jnp.int32, (C, C), 1)
     ).astype(BF16)
-    per_part = 7
     spots = [(i, j) for i in range(3) for j in range(3)]
 
     def turned(values):
         return lax.dot_general(eye, values, (((1,), (1,)), ((), ())), preferred_element_type=F32).astype(BF16)
 
-    def store(g, pair, a, b):
-        part, slot = pair // per_part, pair % per_part
-        both = jnp.concatenate([a.reshape(nz, ny, oc, C), b.reshape(nz, ny, oc, C)], axis=2).astype(BF16)
-        PP[g, part, :, :, slot] = both
-
-    def store_third(g, thirds):
-        thirds = thirds + [jnp.zeros((C, C), F32)]
-        for m in range(5):
-            store(g, 9 + m, thirds[2 * m], thirds[2 * m + 1])
+    groups = ((0, 4), (4, 3))
+
+    def place_of(pair):
+        group = min(pair // 8, 1)
+        base, size = groups[group]
+        at = pair - 8 * group
+        return at // size, base + at % size
+
+    class Taps:
+        def __init__(self, g):
+            self.g, self.held, self.stored, self.sent = g, [], 0, 0
+
+        def add(self, side):
+            self.held.append(side)
+            if len(self.held) == 2:
+                part, slot = place_of(self.stored)
+                a, b = self.held
+                both = jnp.concatenate([a.reshape(nz, ny, oc, C), b.reshape(nz, ny, oc, C)], axis=2)
+                PP[self.g, part, :, :, slot] = both.astype(BF16)
+                self.held = []
+                self.stored += 1
+                if self.stored in (8, 14):
+                    pair_start(self.g, self.sent)
+                    self.sent += 1
 
     def first_kernel_gradient():
         grads = G[0:FR, 1 : 1 + RT].reshape(cells, C).astype(F32)
         for k in range(3):
             LT[k * C : (k + 1) * C] = turned(zero_shift(grads, 1 - k, width).astype(BF16))
-        thirds = []
+        taps = Taps(0)
         for m in range(5):
-            group = spots[2 * m : 2 * m + 2]
-            rhs = jnp.concatenate([X[i : i + FR, j : j + RT].reshape(cells, C) for i, j in group], axis=1)
+            pieces = spots[2 * m : 2 * m + 2]
+            rhs = jnp.concatenate([X[i : i + FR, j : j + RT].reshape(cells, C) for i, j in pieces], axis=1)
             got = jnp.dot(LT[...], rhs, preferred_element_type=F32)
-            for n in range(len(group)):
-                side = got[:, n * C : (n + 1) * C]
-                store(0, 2 * m + n, side[0:C], side[C : 2 * C])
-                thirds.append(side[2 * C : 3 * C])
-        store_third(0, thirds)
+            for n in range(len(pieces)):
+                for k in range(3):
+                    taps.add(got[k * C : (k + 1) * C, n * C : (n + 1) * C])
+        taps.add(jnp.zeros((C, C), F32))
+
+    tall = (RT + 2) * width
+
+    def turn_frame(f):
+        CT[:, f * tall : (f + 1) * tall] = turned(C_[f].reshape(tall, C))
+        CO[:, f * RT * width : (f + 1) * RT * width] = turned(C_[f, 1 : 1 + RT].reshape(RT * width, C))
 
     def second_kernel_gradient():
-        tall = (RT + 2) * width
-        for f in range(FR + 2):
-            CT[:, f * tall : (f + 1) * tall] = turned(C_[f].reshape(tall, C))
-            CO[:, f * RT * width : (f + 1) * RT * width] = turned(C_[f, 1 : 1 + RT].reshape(RT * width, C))
         hidden = H[2 : 2 + FR, 1 : 1 + RT].reshape(cells, C).astype(F32)
         rhs = jnp.concatenate([zero_shift(hidden, k - 1, width).astype(BF16) for k in range(3)], axis=1)
 
@@ -281,46 +296,49 @@
                 [CT[:, f * tall + b * width : f * tall + (b + RT) * width] for f in range(a, a + FR)], axis=1
             )
 
-        thirds = []
+        taps = Taps(1)
         for i in range(3):
             lhs = jnp.concatenate([turned_window(2 - i, 2 - j) for j in range(3)], axis=0)
             got = jnp.dot(lhs, rhs, preferred_element_type=F32)
             for j in range(3):
-                side = got[j * C : (j + 1) * C]
-                store(1, 3 * i + j, side[:, 0:C], side[:, C : 2 * C])
-                thirds.append(side[:, 2 * C : 3 * C])
-        store_third(1, thirds)
-
-    order = list(range(1, nz)) + [0]
-
-    def pair_start(g):
-        copies = []
+                for k in range(3):
+                    taps.add(got[j * C : (j + 1) * C, k * C : (k + 1) * C])
+        taps.add(jnp.zeros((C, C), F32))
+
+    order = [0, 1] + [nz - 1] * (nz > 2) + list(range(2, nz - 1))
+    swaps, planes = {}, {0: [], 1: []}
+
+    def cut(ref, group):
+        base, size = groups[group]
+        return ref.at[:, :, base : base + size]
+
+    def pair_start(g, group):
+        copy = remote(
+            cut(PP.at[g, 1 - core], group), cut(R0.at[g], group), s0.at[g, group], r0.at[g, group], (tm, partner)
+        )
+        swaps[g, group] = copy
+        sent.append(copy)
+
+    def pair_finish(g):
+        for group in range(len(groups)):
+            swaps[g, group].wait_recv()
         for dz in order:
-            at = (z + dz) % nz
-            copies.append(remote(PP.at[g, 1 - core, at], R0.at[g, at], s0.at[g, dz], r0.at[g, dz], (tm, partner)))
-        sent.extend(copies)
-        return copies
-
-    def pair_finish(g, copies):
-        more = []
-        for dz, copy in zip(order, copies):
-            copy.wait_recv()
             at = (z + dz) % nz
             S1[g, at] = (PP[g, core, at].astype(F32) + R0[g, at].astype(F32)).astype(BF16)
             for dy in range(ny):
                 if (dz, dy) == (0, 0):
                     continue
                 e = dz * ny + dy - 1
-                more.append(
-                    remote(S1.at[g, at, (y + dy) % ny], R1.at[g, e], s1.at[g, e], r1.at[g, e], plane_peer(dz, dy))
-                )
-        sent.extend(more)
-        return more
-
+                source = S1.at[g, at, (y + dy) % ny]
+                copy = remote(source, R1.at[g, e], s1.at[g, e], r1.at[g, e], plane_peer(dz, dy))
+                planes[g].append(copy)
+                sent.append(copy)
+
+    last = []
     scale = 1.0 / math.sqrt(cells_all)
 
-    def plane_finish(g, copies):
-        for copy in copies:
+    def plane_finish(g):
+        for copy in planes[g]:
             copy.wait_recv()
         total = S1[g, z, y].astype(F32)
         for e in range(ntm - 1):
@@ -332,8 +350,7 @@
             )
             for o in range(1, nrows)
         ]
-        sent.extend(more)
-        return more
+        last.extend(more)
 
     def give(g, out):
         for o in range(1, nrows):
@@ -344,18 +361,14 @@
                 device_id=(tm, (rows + o) % nrows), device_id_type=MESH,
             ).wait_recv()
         for pair in range(14):
-            part, slot = pair // per_part, pair % per_part
+            part, slot = place_of(pair)
             values = E[g, part, 0, slot].astype(F32)
             for at in range(1, nx):
                 values = values + E[g, part, at, slot].astype(F32)
             values = values * scale
-            if pair < 9:
-                taps = (3 * pair, 3 * pair + 1)
-            else:
-                taps = (6 * (pair - 9) + 2, 6 * (pair - 9) + 5)
-            for n, tap in enumerate(taps):
-                if tap < 27:
-                    out[tap] = values[n * oc : (n + 1) * oc]
+            out[2 * pair] = values[0:oc]
+            if pair < 13:
+                out[2 * pair + 1] = values[oc : 2 * oc]
 
     receive_rows(rows_f, F, True)
     for f in range(2, 2 + FR):
@@ -368,6 +381,8 @@
     receive_rows(rows_c, C_, False)
     arrived("V2")
     early[...] = conv_backward(C_, V2, 0, half)
+    for f in range(FR):
+        turn_frame(f)
 
     receive_time(time_f, F, True)
     for f in range(2):
@@ -378,21 +393,21 @@
     time_g = send_time(3, G, 0, 1, G, False)
 
     receive_time(time_c, C_, False)
+    for f in range(FR, FR + 2):
+        turn_frame(f)
     second_kernel_gradient()
-    pair_b = pair_start(1)
     put(G, half, 1, conv_backward(C_, V2, half, half) * slope[1])
     rows_g = send_rows(3, G, 0, 1, G, False)
-    plane_b = pair_finish(1, pair_b)
+    pair_finish(1)
     first_kernel_gradient()
-    pair_a = pair_start(0)
-    plane_a = pair_finish(0, pair_a)
+    pair_finish(0)
 
     receive_rows(rows_h, H, True)
     receive_time(time_h, H, True)
     arrived("W2")
     put(out_b, 0, 0, get(F, 2, 1, FR) + conv_forward(H, W2, 0, FR))
 
-    rows_b = plane_finish(1, plane_b)
+    plane_finish(1)
 
     receive_rows(rows_g, G, False)
     receive_time(time_g, G, False)
@@ -402,10 +417,12 @@
     turn = sigma * (1.0 + feats * (1.0 - sigma))
     put(out_g, 0, 0, get(C_, 0, 1, FR) + conv_backward(G, V1, 0, FR) * turn)
 
-    rows_a = plane_finish(0, plane_a)
+    plane_finish(0)
+    for copy in sent:
+        copy.wait_send()
     give(1, out_2)
     give(0, out_1)
-    for copy in sent:
+    for copy in last:
         copy.wait_send()
 
 
@@ -445,8 +462,8 @@
         pltpu.SemaphoreType.DMA((50,)),
         pltpu.SemaphoreType.DMA((4, 5)),
         pltpu.SemaphoreType.DMA((4, 5)),
-        pltpu.SemaphoreType.DMA((2, nz)),
-        pltpu.SemaphoreType.DMA((2, nz)),
+        pltpu.SemaphoreType.DMA((2, 3)),
+        pltpu.SemaphoreType.DMA((2, 3)),
         pltpu.SemaphoreType.DMA((2, ntm - 1)),
         pltpu.SemaphoreType.DMA((2, ntm - 1)),
         pltpu.SemaphoreType.DMA((2, 2 * nx - 1)),

time: 41.6 us -> 41.2 us (level)
  no operation moved by 1% of the time
where the time goes in v3:
time: 41.2 us; the launch traced here: 41.1 us
  Pallas kernels  40.4 us (98%)
  between operations  0.64 us (2%)
    pallas_call x1, Pallas kernels, build(): pl.pallas_call(functools.partial(kernel, geom), out_shape=(field, field,...  39.5 us
    pallas_call x1, Pallas kernels, build(): pl.pallas_call(hand_out, out_shape=(field, field, grads, grads), in_specs...  0.89 us

profile of v3, /device:TPU:1, one launch (start us, length us, event | category | flops | bytes accessed | tf_op | source)
XLA Modules:
  0.0 41.1 jit_solution(13812360180985996800)
XLA Ops:
  0.6 39.5 %shard_map.75 = (bf16[4,4,64,128]{3,2,1,0:T(8,128)(2,1)S(1)}, bf16[4,4,64,128]{3,2,1,0:T(8,128)(2,1)S(1)}, f32[27,8,128]{2,1,0:T(8,128)S(1)}, f32[27,8,128]{2,1,0:T(8,128)S(1)}) custom-call(bf16[4,4,64,128]{3,2,1,0:T(8,128)(2,1)} %feat.1, bf16[4,4,64,128]{3,2,1,0:T(8,128)(2,1)} %cot.1, bf16[3,3,3,128,128]{4,3,2,1,0:T(8,128)(2,1)} %k1.1, ...), custom_call_target="tpu_custom_call" | custom-call | tf_op jit(solution)/shard_map/pallas_call | solution.py:479
  40.2 0.9 %shard_map.76 = (bf16[4,4,64,128]{3,2,1,0:T(8,128)(2,1)}, bf16[4,4,64,128]{3,2,1,0:T(8,128)(2,1)}, f32[27,8,128]{2,1,0:T(8,128)}, f32[27,8,128]{2,1,0:T(8,128)}) custom-call(bf16[4,4,64,128]{3,2,1,0:T(8,128)(2,1)S(1)} %get-tuple-element.12.a, bf16[4,4,64,128]{3,2,1,0:T(8,128)(2,1)S(1)} %get-tuple-element.13.b, f32[27,8,128]{2,1,0:T(8,128)S(1)} %get-tuple-element.14.c, ...), custom_call_target="tpu_custom_call" | custom-call | tf_op jit(solution)/shard_map/pallas_call | solution.py:490

commit v4 on v3

--- a/solution.py
+++ b/solution.py
@@ -26,8 +26,8 @@
 
 def kernel(
     geom, feat, cot, k1, k2, out_b, out_g, out_1, out_2,
-    F, X, C_, H, G, W1, V2, W2, V1, slope, early, LT, CT, CO, PP, R0, S1, R1, E,
-    wsem, hsend, hrecv, s0, r0, s1, r1, s2, r2,
+    F, X, C_, H, G, W1, V2, W2, V1, slope, early, LT, CT, CO, PP, R0, S1, S2, A1, A2, E,
+    wsem, hsend, hrecv, s0, r0, s1, r1, s2, r2, s3, r3,
 ):
     nz, ny, nx, width, cells_all = geom
     ntm, nrows = nz * ny, nx * 2
@@ -75,14 +75,13 @@
     load_forward("W2", k2, W2)
     load_backward("V1", k1, V1)
 
-    peers = [(up, right), (up, left), (down, right), (down, left)]
+    peers = [(up, rows), (up, right), (up, left), (down, rows), (down, right), (down, left)]
     peers += [(tm, (rows + o) % nrows) for o in range(1, nrows)]
 
     def plane_peer(dz, dy):
         return (((z + dz) % nz) * ny + (y + dy) % ny, rows)
 
-    offsets = [(dz, dy) for dz in list(range(1, nz)) + [0] for dy in range(ny) if (dz, dy) != (0, 0)]
-    peers += [plane_peer(dz, dy) for dz, dy in offsets]
+    peers += [plane_peer(0, dy) for dy in range(1, ny)] + [plane_peer(dz, 0) for dz in range(1, nz)]
     barrier = pltpu.get_barrier_semaphore()
     for peer in peers:
         pl.semaphore_signal(barrier, inc=1, device_id=peer, device_id_type=MESH)
@@ -192,20 +191,22 @@
             parts.append(jnp.concatenate(blocks, axis=1))
         return jnp.concatenate(parts, axis=0)
 
-    def conv_forward(field, W, lo, count):
-        lhs = window(field, (0, 1, 2), lo, count)
+    def conv_forward(field, W, lo, count, taps=(0, 1, 2)):
+        lhs = window(field, taps, lo, count)
+        deep = len(taps) * 4 * C
         total = None
         for k in (1, 0, 2):
-            got = jnp.dot(lhs, W[k].reshape(12 * C, 2 * C), preferred_element_type=F32)
+            rhs = W[k, taps[0] : taps[-1] + 1].reshape(deep, 2 * C)
+            got = jnp.dot(lhs, rhs, preferred_element_type=F32)
             got = zero_shift(got, k - 1, width)
             total = got if total is None else total + got
         return total
 
-    def conv_backward(field, V, lo, count):
-        lhs = window(field, (2, 1, 0), lo, count)
+    def conv_backward(field, V, lo, count, taps=(0, 1, 2)):
+        lhs = window(field, [2 - i for i in taps], lo, count)
         total = None
         for k in (1, 0, 2):
-            rhs = jnp.concatenate([V[k, i] for i in range(3)], axis=1)
+            rhs = jnp.concatenate([V[k, i] for i in taps], axis=1)
             got = lax.dot_general(lhs, rhs, (((1,), (1,)), ((), ())), preferred_element_type=F32)
             got = zero_shift(got, 1 - k, width)
             total = got if total is None else total + got
@@ -227,7 +228,10 @@
         return jnp.concatenate(parts, axis=0).astype(F32)
 
     def first_conv(part):
-        first_out = conv_forward(X, W1, part * half, half)
+        if part == 0:
+            first_out = conv_forward(X, W1, 0, half, (0, 1)) + early[1]
+        else:
+            first_out = conv_forward(X, W1, half, half)
         sigma = sigmoid(first_out)
         put(H, 2 + part * half, 1, first_out * sigma)
         slope[part] = sigma * (1.0 + first_out * (1.0 - sigma))
@@ -258,6 +262,8 @@
                 part, slot = place_of(self.stored)
                 a, b = self.held
                 both = jnp.concatenate([a.reshape(nz, ny, oc, C), b.reshape(nz, ny, oc, C)], axis=2)
+                if part == 1:
+                    both = jnp.transpose(both, (1, 0, 2, 3))
                 PP[self.g, part, :, :, slot] = both.astype(BF16)
                 self.held = []
                 self.stored += 1
@@ -305,8 +311,7 @@
                     taps.add(got[j * C : (j + 1) * C, k * C : (k + 1) * C])
         taps.add(jnp.zeros((C, C), F32))
 
-    order = [0, 1] + [nz - 1] * (nz > 2) + list(range(2, nz - 1))
-    swaps, planes = {}, {0: [], 1: []}
+    swaps, axes = {}, {0: [], 1: []}
 
     def cut(ref, group):
         base, size = groups[group]
@@ -319,30 +324,46 @@
         swaps[g, group] = copy
         sent.append(copy)
 
-    def pair_finish(g):
+    first, second = (1 - core) * z + core * y, (1 - core) * y + core * z
+
+    def axis_peer(d, turn):
+        along_z = (1 - core) * (1 - turn) + core * turn
+        return (((z + d * along_z) % nz) * ny + (y + d * (1 - along_z)) % ny, rows)
+
+    def axis_start(g):
         for group in range(len(groups)):
             swaps[g, group].wait_recv()
-        for dz in order:
-            at = (z + dz) % nz
+        for d in range(nz):
+            at = (first + nz - d) % nz
             S1[g, at] = (PP[g, core, at].astype(F32) + R0[g, at].astype(F32)).astype(BF16)
-            for dy in range(ny):
-                if (dz, dy) == (0, 0):
-                    continue
-                e = dz * ny + dy - 1
-                source = S1.at[g, at, (y + dy) % ny]
-                copy = remote(source, R1.at[g, e], s1.at[g, e], r1.at[g, e], plane_peer(dz, dy))
-                planes[g].append(copy)
+            if d:
+                copy = remote(S1.at[g, at], A1.at[g, d - 1], s1.at[g, d - 1], r1.at[g, d - 1], axis_peer(nz - d, 0))
+                axes[g].append(copy)
                 sent.append(copy)
+
+    def axis_turn(g):
+        for copy in axes[g]:
+            copy.wait_recv()
+        total = S1[g, first].astype(F32)
+        for d in range(1, nz):
+            total = total + A1[g, d - 1].astype(F32)
+        S2[g] = total.astype(BF16)
+        axes[g] = []
+        for d in range(1, nz):
+            at = (second + d) % nz
+            copy = remote(S2.at[g, at], A2.at[g, d - 1], s3.at[g, d - 1], r3.at[g, d - 1], axis_peer(d, 1))
+            axes[g].append(copy)
+            sent.append(copy)
 
     last = []
     scale = 1.0 / math.sqrt(cells_all)
 
-    def plane_finish(g):
-        for copy in planes[g]:
+    def axes_finish(g):
+        for copy in axes[g]:
             copy.wait_recv()
-        total = S1[g, z, y].astype(F32)
-        for e in range(ntm - 1):
-            total = total + R1[g, e].astype(F32)
+        total = S2[g, second].astype(F32)
+        for d in range(1, nz):
+            total = total + A2[g, d - 1].astype(F32)
         E[g, core, x] = total.astype(BF16)
         more = [
             remote(
@@ -380,7 +401,9 @@
     arrived("C")
     receive_rows(rows_c, C_, False)
     arrived("V2")
-    early[...] = conv_backward(C_, V2, 0, half)
+    early[0] = conv_backward(C_, V2, 0, half)
+    early[1] = conv_forward(X, W1, 0, half, (2,))
+    early[2] = conv_backward(C_, V2, half, half, (2,))
     for f in range(FR):
         turn_frame(f)
 
@@ -389,26 +412,25 @@
         silu_into(f, slice(0, RT + 2))
     first_conv(0)
     rows_h = send_rows(2, H, 2, 1, H, True)
-    put(G, 0, 1, early[...] * slope[0])
+    put(G, 0, 1, early[0] * slope[0])
     time_g = send_time(3, G, 0, 1, G, False)
 
     receive_time(time_c, C_, False)
     for f in range(FR, FR + 2):
         turn_frame(f)
     second_kernel_gradient()
-    put(G, half, 1, conv_backward(C_, V2, half, half) * slope[1])
+    put(G, half, 1, (conv_backward(C_, V2, half, half, (0, 1)) + early[2]) * slope[1])
     rows_g = send_rows(3, G, 0, 1, G, False)
-    pair_finish(1)
+    axis_start(1)
     first_kernel_gradient()
-    pair_finish(0)
-
+    axis_start(0)
+    axis_turn(1)
     receive_rows(rows_h, H, True)
     receive_time(time_h, H, True)
     arrived("W2")
     put(out_b, 0, 0, get(F, 2, 1, FR) + conv_forward(H, W2, 0, FR))
 
-    plane_finish(1)
-
+    axis_turn(0)
     receive_rows(rows_g, G, False)
     receive_time(time_g, G, False)
     arrived("V1")
@@ -417,7 +439,8 @@
     turn = sigma * (1.0 + feats * (1.0 - sigma))
     put(out_g, 0, 0, get(C_, 0, 1, FR) + conv_backward(G, V1, 0, FR) * turn)
 
-    plane_finish(0)
+    axes_finish(1)
+    axes_finish(0)
     for copy in sent:
         copy.wait_send()
     give(1, out_2)
@@ -450,24 +473,28 @@
         pad, pad, pad, pad, pad,
         forward, backward, forward, backward,
         pltpu.VMEM((2, cells // 4, 2 * C), F32),
-        pltpu.VMEM((cells // 4, 2 * C), F32),
+        pltpu.VMEM((3, cells // 4, 2 * C), F32),
         pltpu.VMEM((3 * C, cells), BF16),
         pltpu.VMEM((C, (FR + 2) * (RT + 2) * width), BF16),
         pltpu.VMEM((C, (FR + 2) * RT * width), BF16),
         pltpu.VMEM((2, 2, nz, ny) + block, BF16),
         pltpu.VMEM((2, nz, ny) + block, BF16),
         pltpu.VMEM((2, nz, ny) + block, BF16),
-        pltpu.VMEM((2, ntm - 1) + block, BF16),
+        pltpu.VMEM((2, ny) + block, BF16),
+        pltpu.VMEM((2, nz - 1, ny) + block, BF16),
+        pltpu.VMEM((2, nz - 1) + block, BF16),
         pltpu.VMEM((2, 2, nx) + block, BF16),
         pltpu.SemaphoreType.DMA((50,)),
         pltpu.SemaphoreType.DMA((4, 5)),
         pltpu.SemaphoreType.DMA((4, 5)),
         pltpu.SemaphoreType.DMA((2, 3)),
         pltpu.SemaphoreType.DMA((2, 3)),
-        pltpu.SemaphoreType.DMA((2, ntm - 1)),
-        pltpu.SemaphoreType.DMA((2, ntm - 1)),
+        pltpu.SemaphoreType.DMA((2, nz - 1)),
+        pltpu.SemaphoreType.DMA((2, nz - 1)),
         pltpu.SemaphoreType.DMA((2, 2 * nx - 1)),
         pltpu.SemaphoreType.DMA((2, 2 * nx - 1)),
+        pltpu.SemaphoreType.DMA((2, nz - 1)),
+        pltpu.SemaphoreType.DMA((2, nz - 1)),
     ]
     anywhere = pl.BlockSpec(memory_space=pl.ANY)
     features, cotangent, first_kernel, second_kernel = [

time: 41.2 us -> 40 us (0.971)
  Pallas kernels: 40.4 us -> 39.2 us
    pallas_call x1, Pallas kernels: 39.5 us -> 38.3 us  [build(): pl.pallas_call(functools.partial(kernel, geom), out_shape=(field, field,...]
where the time goes in v4:
time: 40 us; the launch traced here: 39.9 us
  Pallas kernels  39.2 us (98%)
  between operations  0.64 us (2%)
    pallas_call x1, Pallas kernels, build(): pl.pallas_call(functools.partial(kernel, geom), out_shape=(field, field,...  38.3 us
    pallas_call x1, Pallas kernels, build(): pl.pallas_call(hand_out, out_shape=(field, field, grads, grads), in_specs...  0.89 us

profile of v4, /device:TPU:1, one launch (start us, length us, event | category | flops | bytes accessed | tf_op | source)
XLA Modules:
  0.0 39.9 jit_solution(3565477175873546618)
XLA Ops:
  0.6 38.3 %shard_map.75 = (bf16[4,4,64,128]{3,2,1,0:T(8,128)(2,1)S(1)}, bf16[4,4,64,128]{3,2,1,0:T(8,128)(2,1)S(1)}, f32[27,8,128]{2,1,0:T(8,128)S(1)}, f32[27,8,128]{2,1,0:T(8,128)S(1)}) custom-call(bf16[4,4,64,128]{3,2,1,0:T(8,128)(2,1)} %feat.1, bf16[4,4,64,128]{3,2,1,0:T(8,128)(2,1)} %cot.1, bf16[3,3,3,128,128]{4,3,2,1,0:T(8,128)(2,1)} %k1.1, ...), custom_call_target="tpu_custom_call" | custom-call | tf_op jit(solution)/shard_map/pallas_call | solution.py:506
  39.0 0.9 %shard_map.76 = (bf16[4,4,64,128]{3,2,1,0:T(8,128)(2,1)}, bf16[4,4,64,128]{3,2,1,0:T(8,128)(2,1)}, f32[27,8,128]{2,1,0:T(8,128)}, f32[27,8,128]{2,1,0:T(8,128)}) custom-call(bf16[4,4,64,128]{3,2,1,0:T(8,128)(2,1)S(1)} %get-tuple-element.12.a, bf16[4,4,64,128]{3,2,1,0:T(8,128)(2,1)S(1)} %get-tuple-element.13.b, f32[27,8,128]{2,1,0:T(8,128)S(1)} %get-tuple-element.14.c, ...), custom_call_target="tpu_custom_call" | custom-call | tf_op jit(solution)/shard_map/pallas_call | solution.py:517

commit v5 on v4

--- a/solution.py
+++ b/solution.py
@@ -425,12 +425,13 @@
     first_kernel_gradient()
     axis_start(0)
     axis_turn(1)
+    axis_turn(0)
     receive_rows(rows_h, H, True)
     receive_time(time_h, H, True)
     arrived("W2")
     put(out_b, 0, 0, get(F, 2, 1, FR) + conv_forward(H, W2, 0, FR))
 
-    axis_turn(0)
+    axes_finish(1)
     receive_rows(rows_g, G, False)
     receive_time(time_g, G, False)
     arrived("V1")
@@ -439,7 +440,6 @@
     turn = sigma * (1.0 + feats * (1.0 - sigma))
     put(out_g, 0, 0, get(C_, 0, 1, FR) + conv_backward(G, V1, 0, FR) * turn)
 
-    axes_finish(1)
     axes_finish(0)
     for copy in sent:
         copy.wait_send()

time: 40 us -> 40 us (level)
  no operation moved by 1% of the time
where the time goes in v5:
time: 40 us; the launch traced here: 39.9 us
  Pallas kernels  39.2 us (98%)
  between operations  0.64 us (2%)
    pallas_call x1, Pallas kernels, build(): pl.pallas_call(functools.partial(kernel, geom), out_shape=(field, field,...  38.3 us
    pallas_call x1, Pallas kernels, build(): pl.pallas_call(hand_out, out_shape=(field, field, grads, grads), in_specs...  0.89 us

profile of v5, /device:TPU:1, one launch (start us, length us, event | category | flops | bytes accessed | tf_op | source)
XLA Modules:
  0.0 39.9 jit_solution(15598880890829042569)
XLA Ops:
  0.6 38.3 %shard_map.75 = (bf16[4,4,64,128]{3,2,1,0:T(8,128)(2,1)S(1)}, bf16[4,4,64,128]{3,2,1,0:T(8,128)(2,1)S(1)}, f32[27,8,128]{2,1,0:T(8,128)S(1)}, f32[27,8,128]{2,1,0:T(8,128)S(1)}) custom-call(bf16[4,4,64,128]{3,2,1,0:T(8,128)(2,1)} %feat.1, bf16[4,4,64,128]{3,2,1,0:T(8,128)(2,1)} %cot.1, bf16[3,3,3,128,128]{4,3,2,1,0:T(8,128)(2,1)} %k1.1, ...), custom_call_target="tpu_custom_call" | custom-call | tf_op jit(solution)/shard_map/pallas_call | solution.py:506
  39.0 0.9 %shard_map.76 = (bf16[4,4,64,128]{3,2,1,0:T(8,128)(2,1)}, bf16[4,4,64,128]{3,2,1,0:T(8,128)(2,1)}, f32[27,8,128]{2,1,0:T(8,128)}, f32[27,8,128]{2,1,0:T(8,128)}) custom-call(bf16[4,4,64,128]{3,2,1,0:T(8,128)(2,1)S(1)} %get-tuple-element.12.a, bf16[4,4,64,128]{3,2,1,0:T(8,128)(2,1)S(1)} %get-tuple-element.13.b, f32[27,8,128]{2,1,0:T(8,128)S(1)} %get-tuple-element.14.c, ...), custom_call_target="tpu_custom_call" | custom-call | tf_op jit(solution)/shard_map/pallas_call | solution.py:517
